TPU v7x, 32 devices: a whole 2x2x4 slice. The times are simulated.
32 devices in a mesh: group: 2 (over y), dp: 8 (over z, x), shard: 2 (over core).
Axes of the slice: x: 2, y: 2, z: 4, core: 2. Of those that a mesh axis runs over, the one named last changes fastest.
Arguments:
- inputs: bfloat16 [32, 16, 32, 256], P(('group', 'dp', 'shard')), parts along dimension 0, may hold values from -6 to 6
- cotangent: bfloat16 [32, 16, 32, 256], P(('group', 'dp', 'shard')), parts along dimension 0, may hold values from -6 to 6
- conv_first: bfloat16 [18, 256, 256], P('group', None, 'shard'), parts along dimension 0, may hold values from -0.125 to 0.125
- conv_second: bfloat16 [18, 256, 256], P('group', None, 'shard'), parts along dimension 0, may hold values from -0.125 to 0.125
Outputs:
- outputs: bfloat16 [32, 16, 32, 256], P(('group', 'dp', 'shard')), parts along dimension 0
- grad_first: bfloat16 [18, 256, 256], P('group', None, 'shard'), parts along dimension 0
- grad_second: bfloat16 [18, 256, 256], P('group', None, 'shard'), parts along dimension 0
There are 2 independent parts, one for each index of `group`. A program takes and returns all parts, laid end to end along the dimension named above; each array names one. Nothing has to cross between parts.
All inputs are finite; a program needn't handle non-finite values.
Results may differ from a plain program's by a relative error of at most 0.012.
Values may be sent and summed in bfloat16 or wider, within the bound.
No kernel may reach another device: no remote copies, remote signals or barrier semaphores. Data moves between devices by JAX's collectives and lax.ppermute only.
A program may use at most 64 MiB of HBM per device.

v0:
```python
import jax
import jax.numpy as jnp
from jax import lax
from jax.sharding import PartitionSpec as P


def conv_taps(field, kernel):
    samples, rows, cols, chans = field.shape
    padded = jnp.pad(field, ((0, 0), (1, 1), (1, 1), (0, 0)))
    total = jnp.zeros((samples * rows * cols, kernel.shape[2]), jnp.float32)
    for tap in range(9):
        above = tap // 3
        left = tap % 3
        window = padded[:, above : above + rows, left : left + cols, :].reshape(-1, chans)
        total = total + jnp.dot(window, kernel[tap], preferred_element_type=jnp.float32)
    return total.reshape(samples, rows, cols, kernel.shape[2])


def flipped(kernel):
    return jnp.transpose(kernel[::-1], (0, 2, 1))


def weight_terms(field, grad):
    samples, rows, cols, chans = field.shape
    padded = jnp.pad(field, ((0, 0), (1, 1), (1, 1), (0, 0)))
    grad_flat = grad.reshape(-1, grad.shape[3])
    terms = []
    for tap in range(9):
        above = tap // 3
        left = tap % 3
        window = padded[:, above : above + rows, left : left + cols, :].reshape(-1, chans)
        terms.append(
            lax.dot_general(
                window, grad_flat, (((0,), (0,)), ((), ())), preferred_element_type=jnp.float32
            )
        )
    return jnp.stack(terms, 0)


def body(inputs, cotangent, conv_first, conv_second):
    pre = conv_taps(inputs, lax.all_gather(conv_first, "shard", axis=2, tiled=True))
    hidden = jax.nn.silu(pre).astype(jnp.bfloat16)
    outputs = (
        inputs.astype(jnp.float32)
        + conv_taps(hidden, lax.all_gather(conv_second, "shard", axis=2, tiled=True))
    ).astype(jnp.bfloat16)
    back = conv_taps(cotangent, flipped(lax.all_gather(conv_second, "shard", axis=2, tiled=True)))
    sigma = jax.nn.sigmoid(pre)
    dpre = (back * sigma * (1.0 + pre * (1.0 - sigma))).astype(jnp.bfloat16)
    scale = 1.0 / (inputs.shape[0] * lax.axis_size("dp") * lax.axis_size("shard"))
    second_part = weight_terms(hidden, cotangent)
    first_part = weight_terms(inputs, dpre)
    first_half, second_half = (
        lax.psum_scatter(
            first_part.astype(jnp.bfloat16), "shard", scatter_dimension=2, tiled=True
        ).astype(jnp.float32),
        lax.psum_scatter(
            second_part.astype(jnp.bfloat16), "shard", scatter_dimension=2, tiled=True
        ).astype(jnp.float32),
    )
    first_sum, second_sum = lax.psum((first_half, second_half), "dp")
    grad_first = (first_sum * scale).astype(jnp.bfloat16)
    grad_second = (second_sum * scale).astype(jnp.bfloat16)
    return (outputs, grad_first, grad_second)


def solution(mesh):
    placed = (
        P(("group", "dp", "shard"), None, None, None),
        P(("group", "dp", "shard"), None, None, None),
        P("group", None, "shard"),
        P("group", None, "shard"),
    )
    return jax.shard_map(
        body,
        mesh=mesh,
        in_specs=placed,
        out_specs=(
            P(("group", "dp", "shard"), None, None, None),
            P("group", None, "shard"),
            P("group", None, "shard"),
        ),
        check_vma=False,
    )
```

profile of v0, /device:TPU:0, one launch (start us, length us, event | category | flops | bytes accessed | tf_op | source)
XLA Modules:
  0.0 177.9 jit_solution(16371178094781244886)
XLA Ops:
  7.2 0.7 all-gather.5.cloned.1.call-update
  8.0 0.7 all-gather.3.cloned.1.call-update
  8.7 1.1 pad_slice_fusion.16
  9.8 1.4 pad_slice_fusion
  11.2 10.2 %all-gather.5.cloned.1.call-done = bf16[9,256,256]{2,1,0:T(8,128)(2,1)} async-done(((bf16[9,256,128]{2,1,0:T(8,128)(2,1)}), bf16[9,256,256]{2,1,0:T(8,128)(2,1)}) %all-gather.5.cloned.1.call-update) | async-done | bytes 1179664 | tf_op jit(solution)/shard_map/all_gather | solution.py:45
  21.4 1.4 reverse_bitcast_fusion
  23.4 0.4 copy-done.11
  24.6 0.4 copy-done.9
  25.6 0.4 copy-done.7
  26.0 1.0 convolution_add_fusion.1
  27.1 6.3 %all-gather.3.cloned.1.call-done = bf16[9,256,256]{2,1,0:T(8,128)(2,1)} async-done(((bf16[9,256,128]{2,1,0:T(8,128)(2,1)}), bf16[9,256,256]{2,1,0:T(8,128)(2,1)}) %all-gather.3.cloned.1.call-update) | async-done | bytes 1179664 | tf_op jit(solution)/shard_map/all_gather | solution.py:41
  33.4 1.2 fusion.85
  34.6 1.1 convolution_add_fusion.23
  37.1 0.5 copy-done.17
  37.6 1.0 multiply_convert_fusion.2
  38.7 0.4 fusion.2
  42.0 2.2 %copy.11 = bf16[9,256,256]{1,0,2:T(8,128)(2,1)S(1)} copy(bf16[9,256,256]{2,1,0:T(8,128)(2,1)S(1)} %fusion.40) | data formatting | bytes 2359296
  44.1 1.6 copy.15
  46.0 0.8 copy-done.15
  48.1 0.7 copy-done.19
  50.1 2.2 %copy.13 = bf16[9,256,256]{1,0,2:T(8,128)(2,1)S(1)} copy(bf16[9,256,256]{2,1,0:T(8,128)(2,1)S(1)} %fusion.22) | data formatting | bytes 2359296
  52.3 1.5 copy.16
  54.2 1.3 copy-done
  56.5 0.5 copy-done.20
  58.1 0.8 add_convert_fusion
  58.9 1.4 reshape.326
  60.3 0.8 copy.12
  61.2 6.6 %reduce-scatter.9.cloned.1.call-done = bf16[128,2304]{1,0:T(8,128)(2,1)} async-done(((bf16[256,2304]{1,0:T(8,128)(2,1)}), bf16[128,2304]{1,0:T(8,128)(2,1)}) %reduce-scatter.9.cloned.1.call-update) | async-done | bytes 589840
  67.8 1.4 reshape.328
  69.2 0.8 copy.14
  70.0 98.7 %all-reduce.5 = (f32[9,256,128]{2,1,0:T(8,128)S(1)}, f32[9,256,128]{2,1,0:T(8,128)}) all-reduce(bf16[9,256,128]{2,1,0:T(8,128)(2,1)S(1)} %copy.12, bf16[9,256,128]{2,1,0:T(8,128)(2,1)S(1)} %copy.14), channel_id=1, replica_groups=mesh['group'=2,'dp'=8,'shard'=2] {'dp'}, use_global_device_ids=true, to_apply=%region_1.2 | all-reduce | flops 589824 | bytes 3538944 | tf_op jit(solution)/shard_map/psum | solution.py:61
  168.8 2.5 %multiply_convert_fusion = (bf16[9,256,128]{2,1,0:T(8,128)(2,1)}, bf16[9,256,128]{2,1,0:T(8,128)(2,1)}) fusion(f32[9,256,128]{2,1,0:T(8,128)} %get-tuple-element.4, f32[9,256,128]{2,1,0:T(8,128)S(1)} %get-tuple-element.3), kind=kLoop, calls=%fused_computation.27 | loop fusion | flops 1179648 | bytes 3538944 | tf_op jit(solution)/shard_map/convert_element_type | solution.py:63
  (83 shorter events, 11.5 us)
Async XLA Ops:
  7.2 1.6 copy-start.1
  7.2 14.3 %all-gather.5.cloned.1.call-start = ((), (), s32[]{:S(2)}) async-start(), calls=%async_computation.3 | async-start | bytes 1769472 | tf_op jit(solution)/shard_map/all_gather | solution.py:45
  7.9 25.5 %all-gather.3.cloned.1.call-start = ((), (), s32[]{:S(2)}) async-start(), calls=%async_computation.2 | async-start | bytes 1769472 | tf_op jit(solution)/shard_map/all_gather | solution.py:41
  8.7 1.2 copy-start.4
  8.7 50.3 %reduce-scatter.7.cloned.1.call-start = ((), (), s32[]{:S(2)}) async-start(), calls=%async_computation.4 | async-start | bytes 1769472
  21.4 1.7 copy-start.12
  22.8 1.0 copy-start.11
  23.1 1.0 copy-start.10
  24.1 0.9 copy-start.9
  24.3 1.0 copy-start.8
  25.0 1.0 copy-start.7
  26.0 8.6 %copy-start.6 = (bf16[1,16,32,256]{3,2,1,0:T(8,128)(2,1)S(1)}, bf16[1,16,32,256]{3,2,1,0:T(8,128)(2,1)}, u32[]{:S(2)}) copy-start(bf16[1,16,32,256]{3,2,1,0:T(8,128)(2,1)} %get-tuple-element.22) | copy-start | bytes 786436
  33.4 2.4 %copy-start.13 = (bf16[9,256,256]{2,1,0:T(8,128)(2,1)S(1)}, bf16[9,256,256]{2,1,0:T(8,128)(2,1)}, u32[]{:S(2)}) copy-start(bf16[9,256,256]{2,1,0:T(8,128)(2,1)} %all-gather.3.cloned.1.call-done) | copy-start | bytes 3538948
  36.7 1.0 copy-start.17
  37.6 1.0 copy-start.16
  37.6 1.1 copy-start.18
  38.7 0.8 copy-start.14
  45.7 1.0 copy-start.15
  45.7 1.2 copy-start.5
  45.7 22.1 %reduce-scatter.9.cloned.1.call-start = ((), (), s32[]{:S(2)}) async-start(), calls=%async_computation.5 | async-start | bytes 1769472
  46.9 2.9 %copy-start.2 = (bf16[1,16,32,256]{3,2,1,0:T(8,128)(2,1)}, bf16[1,16,32,256]{3,2,1,0:T(8,128)(2,1)S(1)}, u32[]{:S(2)}) copy-start(bf16[1,16,32,256]{3,2,1,0:T(8,128)(2,1)S(1)} %multiply_convert_fusion.3) | copy-start | bytes 786436
  47.8 1.0 copy-start.19
  52.3 1.6 copy-start.3
  54.2 1.3 copy-start
  56.0 1.0 copy-start.20
Sparse Core Ops, SparseCore 0:
  9.5 11.8 all-gather.4
  23.0 10.3 all-gather.2
  45.9 9.8 reduce-scatter.6
  57.9 9.8 reduce-scatter.8
where the time goes:
time: 178 us
  blocking collectives  98.7 us (55%)
  waiting for transfers between devices  24.6 us (14%)
  local copies, waits for them, and re-layouts  21.6 us (12%)
  matrix products  14.9 us (8%)
  between operations  14.2 us (8%)
  other arithmetic  3.46 us (2%)
    psum x1, blocking collectives, body(): first_sum, second_sum = lax.psum((first_half, second_half), 'dp')  98.7 us
    unnamed x50, local copies, waits for them, and re-layouts  17.4 us
    all_gather x1, waiting for transfers between devices, body(): lax.all_gather(conv_second, 'shard', axis=2, tiled=True)  10.2 us
    dot_general x27, matrix products, conv_taps(): jnp.dot(window, kernel[tap], preferred_element_type=jnp.float32)  9.95 us
    unnamed x6, waiting for transfers between devices  8.06 us
    all_gather x1, waiting for transfers between devices, body(): lax.all_gather(conv_first, 'shard', axis=2, tiled=True)  6.31 us
    dot_general x18, matrix products, weight_terms(): lax.dot_general(window, grad_flat, (((0,), (0,)), ((), ())), preferred_el...  4.97 us
  transfers between devices with their start and end apart: 4, of which 3 were waited for; matrix products, arithmetic and copies ran while one was open for 10% of the time, Pallas kernels for 0%

commit v1 on v0

v1 whole, which is shorter than its diff:
```python
import functools

import jax
import jax.numpy as jnp
from jax import lax
from jax.experimental import pallas as pl
from jax.experimental.pallas import tpu as pltpu
from jax.sharding import PartitionSpec as P

F32 = jnp.float32
BF16 = jnp.bfloat16
VMEM_LIMIT = 40 * 1024 * 1024


def column_shifted(field, cols, by):
    cells = field.shape[0]
    col = lax.broadcasted_iota(jnp.int32, field.shape, 0) % cols
    if by == 0:
        return field
    rolled = pltpu.roll(field, (-by) % cells, 0)
    return jnp.where(col == (cols - 1 if by > 0 else 0), 0.0, rolled)


def fill_taps(dst, field, cols, order):
    cells, chans = field.shape
    zeros = jnp.zeros((cols, dst.shape[1]), dst.dtype)
    dst[0:cols, :] = zeros
    dst[cols + cells : cols + cells + cols, :] = zeros
    for slot, by in enumerate(order):
        dst[cols : cols + cells, slot * chans : (slot + 1) * chans] = column_shifted(
            field, cols, by
        ).astype(dst.dtype)


def join_halves(dst, own, other, half, start, away):
    dst[:, pl.ds(start, half)] = own[...]
    dst[:, pl.ds(away, half)] = other[...]


def place(half):
    mine = lax.axis_index("shard")
    start = pl.multiple_of(mine * half, half)
    away = pl.multiple_of((1 - mine) * half, half)
    return start, away


def first_kernel(
    cols, x_own, x_other, c_own, c_other, w_own, w_other,
    grad_ref, hidden_ref, slope_ref,
    weight, taps, narrow, turned, pre_ref,
):
    cells, chans = x_own.shape
    half = w_own.shape[1]
    start, away = place(half)
    join_halves(weight, w_own, w_other, half, start, away)
    for sample, (x_ref, c_ref) in enumerate(((x_own, c_own), (x_other, c_other))):
        fill_taps(taps, x_ref[...].astype(F32), cols, (-1, 0, 1))
        pre = jnp.zeros((cells, chans), F32)
        for above in range(3):
            pre = pre + jnp.dot(
                taps[above * cols : above * cols + cells, :],
                weight[above * 3 * chans : (above + 1) * 3 * chans, :],
                preferred_element_type=F32,
            )
        pre_ref[...] = pre
        hidden = pre * jax.nn.sigmoid(pre)
        if sample == 0:
            hidden_ref[...] = hidden.astype(BF16)
        turned[:, sample * cells : (sample + 1) * cells] = hidden.T.astype(BF16)
        mine = pre_ref[:, pl.ds(start, half)]
        sg = jax.nn.sigmoid(mine)
        slope_ref[sample * cells : (sample + 1) * cells, :] = sg * (1.0 + mine * (1.0 - sg))
        fill_taps(narrow.at[sample], c_ref[:, pl.ds(start, half)].astype(F32), cols, (1, 0, -1))
    weight_grad(cols, turned, narrow, grad_ref)


def weight_grad(cols, turned, narrow, grad_ref):
    chans = turned.shape[0]
    half = grad_ref.shape[1]
    cells = turned.shape[1] // 2
    for above in range(3):
        at = (2 - above) * cols
        part = jnp.zeros((chans, 3 * half), F32)
        for sample in range(2):
            part = part + jnp.dot(
                turned[:, sample * cells : (sample + 1) * cells],
                narrow[sample, at : at + cells, :],
                preferred_element_type=F32,
            )
        for left in range(3):
            tap = 3 * above + left
            grad_ref[tap * chans : (tap + 1) * chans, :] = part[
                :, left * half : (left + 1) * half
            ].astype(BF16)


def second_kernel(
    cols, x_own, x_other, c_own, c_other, w_own, w_other, slope_ref,
    grad_ref,
    weight, taps, narrow, turned,
):
    cells, chans = x_own.shape
    half = w_own.shape[1]
    start, away = place(half)
    join_halves(weight, w_own, w_other, half, start, away)
    for sample, (x_ref, c_ref) in enumerate(((x_own, c_own), (x_other, c_other))):
        fill_taps(taps, c_ref[...].astype(F32), cols, (1, 0, -1))
        turned[:, sample * cells : (sample + 1) * cells] = x_ref[...].astype(F32).T.astype(BF16)
        back = jnp.zeros((cells, half), F32)
        for tap in range(9):
            above, left = tap // 3, tap % 3
            at = (2 - above) * cols
            back = back + lax.dot_general(
                taps[at : at + cells, left * chans : (left + 1) * chans],
                weight[pl.ds(pl.multiple_of(tap * chans + start, half), half), :],
                (((1,), (1,)), ((), ())),
                preferred_element_type=F32,
            )
        dpre = back * slope_ref[sample * cells : (sample + 1) * cells, :]
        fill_taps(narrow.at[sample], dpre, cols, (1, 0, -1))
    weight_grad(cols, turned, narrow, grad_ref)


def output_kernel(cols, x_ref, h_ref, w_own, w_other, out_ref, weight, taps):
    cells, chans = x_ref.shape
    half = w_own.shape[1]
    start, away = place(half)
    join_halves(weight, w_own, w_other, half, start, away)
    fill_taps(taps, h_ref[...].astype(F32), cols, (-1, 0, 1))
    total = x_ref[...].astype(F32)
    for above in range(3):
        total = total + jnp.dot(
            taps[above * cols : above * cols + cells, :],
            weight[above * 3 * chans : (above + 1) * 3 * chans, :],
            preferred_element_type=F32,
        )
    out_ref[...] = total.astype(BF16)


def call(kernel, cols, outs, scratch, flops, *args):
    moved = sum(a.size * a.dtype.itemsize for a in args)
    return pl.pallas_call(
        functools.partial(kernel, cols),
        out_shape=outs,
        in_specs=[pl.BlockSpec(memory_space=pltpu.VMEM)] * len(args),
        out_specs=jax.tree.map(lambda _: pl.BlockSpec(memory_space=pltpu.VMEM), outs),
        scratch_shapes=scratch,
        compiler_params=pltpu.CompilerParams(vmem_limit_bytes=VMEM_LIMIT),
        cost_estimate=pl.CostEstimate(flops=flops, bytes_accessed=moved, transcendentals=0),
    )(*args)


def cube_orders(bits):
    plain = list(range(bits))
    return plain, ([1, 0] + plain[2:] if bits > 2 else plain)


def cube_swap(value, orders, step):
    devices = lax.axis_size("dp")
    pairs = [
        (2 * d + c, 2 * (d ^ (1 << orders[c][step])) + c) for d in range(devices) for c in range(2)
    ]
    return lax.ppermute(value, ("dp", "shard"), pairs)


def cube_bit(orders, step):
    core = lax.axis_index("shard")
    return (lax.axis_index("dp") >> jnp.where(core == 0, orders[0][step], orders[1][step])) & 1


def summed_over_dp(value, scale):
    devices = lax.axis_size("dp")
    bits = devices.bit_length() - 1
    if devices != 1 << bits or bits == 0 or value.shape[0] % (1 << (bits - 1)):
        return (lax.psum(value.astype(F32), "dp") * scale).astype(BF16)
    orders = cube_orders(bits)
    for step in range(bits - 1):
        half = value.shape[0] // 2
        bit = cube_bit(orders, step)
        sent = lax.dynamic_slice_in_dim(value, (1 - bit) * half, half, 0)
        kept = lax.dynamic_slice_in_dim(value, bit * half, half, 0)
        came = cube_swap(sent, orders, step)
        value = (kept.astype(F32) + came.astype(F32)).astype(BF16)
    came = cube_swap(value, orders, bits - 1)
    value = ((value.astype(F32) + came.astype(F32)) * scale).astype(BF16)
    for step in range(bits - 2, -1, -1):
        came = cube_swap(value, orders, step)
        bit = cube_bit(orders, step)
        value = jnp.where(
            bit == 0,
            jnp.concatenate([value, came], 0),
            jnp.concatenate([came, value], 0),
        )
    return value


def body(inputs, cotangent, conv_first, conv_second):
    _, rows, cols, chans = inputs.shape
    cells = rows * cols
    half = conv_first.shape[2]
    swap = [(0, 1), (1, 0)]
    x_own = inputs.reshape(cells, chans)
    c_own = cotangent.reshape(cells, chans)
    w1_own = conv_first.reshape(9 * chans, half)
    w2_own = conv_second.reshape(9 * chans, half)
    w1_other, x_other, c_other, w2_other = (
        lax.ppermute(v, "shard", swap) for v in (w1_own, x_own, c_own, w2_own)
    )
    unit = 2 * 9 * cells * chans * chans
    weight = pltpu.VMEM((9 * chans, chans), BF16)
    taps = pltpu.VMEM((cells + 2 * cols, 3 * chans), BF16)
    narrow = pltpu.VMEM((2, cells + 2 * cols, 3 * half), BF16)
    turned = pltpu.VMEM((chans, 2 * cells), BF16)
    grad_shape = jax.ShapeDtypeStruct((9 * chans, half), BF16)
    second, hidden, slope = call(
        first_kernel,
        cols,
        (
            grad_shape,
            jax.ShapeDtypeStruct((cells, chans), BF16),
            jax.ShapeDtypeStruct((2 * cells, half), F32),
        ),
        [weight, taps, narrow, turned, pltpu.VMEM((cells, chans), F32)],
        3 * unit,
        x_own, x_other, c_own, c_other, w1_own, w1_other,
    )
    first = call(
        second_kernel,
        cols,
        grad_shape,
        [weight, taps, narrow, turned],
        2 * unit,
        x_own, x_other, c_own, c_other, w2_own, w2_other, slope,
    )
    outputs = call(
        output_kernel,
        cols,
        jax.ShapeDtypeStruct((cells, chans), BF16),
        [weight, taps],
        unit,
        x_own, hidden, w2_own, w2_other,
    )
    scale = 1.0 / (inputs.shape[0] * lax.axis_size("dp") * lax.axis_size("shard"))
    grad_second = summed_over_dp(second, scale)
    grad_first = summed_over_dp(first, scale)
    return (
        outputs.reshape(inputs.shape),
        grad_first.reshape(conv_first.shape),
        grad_second.reshape(conv_second.shape),
    )


def solution(mesh):
    placed = (
        P(("group", "dp", "shard"), None, None, None),
        P(("group", "dp", "shard"), None, None, None),
        P("group", None, "shard"),
        P("group", None, "shard"),
    )
    return jax.shard_map(
        body,
        mesh=mesh,
        in_specs=placed,
        out_specs=(
            P(("group", "dp", "shard"), None, None, None),
            P("group", None, "shard"),
            P("group", None, "shard"),
        ),
        check_vma=False,
    )
```

time: 178 us -> 59 us (0.33)
  blocking collectives: 98.7 us -> 0 us
  starting transfers between devices: 0.34 us -> 19.5 us
  local copies, waits for them, and re-layouts: 21.6 us -> 3.06 us
  matrix products: 14.9 us -> 0 us
  between operations: 14.2 us -> 0.75 us
  Pallas kernels: 0 us -> 7.26 us
    psum x1 -> x0, blocking collectives: 98.7 us -> none  [body(): first_sum, second_sum = lax.psum((first_half, second_half), 'dp')]
    ppermute x0 -> x14, waiting for transfers between devices: none -> 25.7 us  [the longest x10 22.9 us: cube_swap(): return lax.ppermute(value, ('dp', 'shard'), pairs)]
    ppermute x0 -> x14, starting transfers between devices: none -> 19.5 us  [the longest x10 18.4 us: cube_swap(): return lax.ppermute(value, ('dp', 'shard'), pairs)]
    all_gather x2 -> x0, waiting for transfers between devices: 16.5 us -> none  [the longest x1 10.2 us: body(): lax.all_gather(conv_second, 'shard', axis=2, tiled=True)]
    dot_general x45 -> x0, matrix products: 14.9 us -> none  [the longest x27 9.95 us: conv_taps(): jnp.dot(window, kernel[tap], preferred_element_type=jnp.float32)]
    unnamed x50 -> x10, local copies, waits for them, and re-layouts: 17.4 us -> 2.97 us
    unnamed x6 -> x0, waiting for transfers between devices: 8.06 us -> none
    pallas_call x0 -> x3, Pallas kernels: none -> 7.26 us  [call(): pl.pallas_call(functools.partial(kernel, cols), out_shape=outs, in_specs=...]
  transfers between devices with their start and end apart: 4 -> 14, of which waited for: 3 -> 10; matrix products, arithmetic and copies ran while one was open for 10% -> 3% of each run, Pallas kernels for 0% -> 8%
where the time goes in v1:
time: 59 us; the launch traced here: 58.7 us
  waiting for transfers between devices  25.7 us (44%)
  starting transfers between devices  19.5 us (33%)
  Pallas kernels  7.26 us (12%)
  local copies, waits for them, and re-layouts  3.06 us (5%)
  other arithmetic  2.48 us (4%)
  between operations  0.75 us (1%)
    ppermute x10, waiting for transfers between devices, cube_swap(): return lax.ppermute(value, ('dp', 'shard'), pairs)  22.9 us
    ppermute x10, starting transfers between devices, cube_swap(): return lax.ppermute(value, ('dp', 'shard'), pairs)  18.4 us
    pallas_call x3, Pallas kernels, call(): pl.pallas_call(functools.partial(kernel, cols), out_shape=outs, in_specs=...  7.26 us
    unnamed x10, local copies, waits for them, and re-layouts  2.97 us
    ppermute x4, waiting for transfers between devices, body(): lax.ppermute(v, 'shard', swap)  2.85 us
    select_n x4, other arithmetic, summed_over_dp(): jnp.where(bit == 0, jnp.concatenate([value, came], 0), jnp.concatenate([c...  2.13 us
  transfers between devices with their start and end apart: 14, of which 10 were waited for; matrix products, arithmetic and copies ran while one was open for 3% of the time, Pallas kernels for 8%

profile of v1, /device:TPU:0, one launch (start us, length us, event | category | flops | bytes accessed | tf_op | source)
XLA Modules:
  0.0 58.7 jit_solution(11154017309974852001)
XLA Ops:
  0.6 0.5 collective-permute-start.2
  1.2 0.4 collective-permute-start
  1.7 2.5 %collective-permute-done.x_other = bf16[512,256]{1,0:T(8,128)(2,1)S(1)} collective-permute-done((bf16[512,256]{1,0:T(8,128)(2,1)}, bf16[512,256]{1,0:T(8,128)(2,1)S(1)}, u32[]{:S(2)}, u32[]{:S(2)}) %collective-permute-start) | collective-permute-done | bytes 262176 | tf_op jit(solution)/shard_map/ppermute | solution.py:207
  4.2 0.4 collective-permute-done.1.c_other
  4.6 1.1 %copy-done = bf16[9,256,128]{2,1,0:T(8,128)(2,1)S(1)} copy-done((bf16[9,256,128]{2,1,0:T(8,128)(2,1)S(1)}, bf16[9,256,128]{2,1,0:T(8,128)(2,1)}, u32[]{:S(2)}) %copy-start) | copy-done | bytes 589848
  5.7 0.9 %copy-done.2 = bf16[1,16,32,256]{3,2,1,0:T(8,128)(2,1)S(1)} copy-done((bf16[1,16,32,256]{3,2,1,0:T(8,128)(2,1)S(1)}, bf16[1,16,32,256]{3,2,1,0:T(8,128)(2,1)}, u32[]{:S(2)}) %copy-start.2) | copy-done | bytes 262168
  6.6 0.9 %copy-done.3 = bf16[1,16,32,256]{3,2,1,0:T(8,128)(2,1)S(1)} copy-done((bf16[1,16,32,256]{3,2,1,0:T(8,128)(2,1)S(1)}, bf16[1,16,32,256]{3,2,1,0:T(8,128)(2,1)}, u32[]{:S(2)}) %copy-start.3) | copy-done | bytes 262168
  7.6 2.9 %shard_map.67 = (bf16[2304,128]{1,0:T(8,128)(2,1)S(1)}, bf16[512,256]{1,0:T(8,128)(2,1)S(1)}, f32[1024,128]{1,0:T(8,128)S(1)}) custom-call(bf16[512,256]{1,0:T(8,128)(2,1)S(1)} %bitcast.16, bf16[512,256]{1,0:T(8,128)(2,1)S(1)} %collective-permute-done.x_other, bf16[512,256]{1,0:T(8,128)(2,1)S(1)} %bitcast.13, ...), custom_call_target="tpu_custom_call" | custom-call | flops 1811939328 | bytes 2228224 | tf_op jit(solution)/shard_map/pallas_call | solution.py:142
  10.5 2.5 %shard_map.69 = bf16[2304,128]{1,0:T(8,128)(2,1)S(1)} custom-call(bf16[512,256]{1,0:T(8,128)(2,1)S(1)} %bitcast.17, bf16[512,256]{1,0:T(8,128)(2,1)S(1)} %collective-permute-done.x_other, bf16[512,256]{1,0:T(8,128)(2,1)S(1)} %bitcast.14, bf16[512,256]{1,0:T(8,128)(2,1)S(1)} %collective-permute-done.1.c_other, bf16[2304,128]{1,0:T(8,128)(2,1)S(1)} %bitcast.10, ...), custom_call_target="tpu_custom_call" | custom-call | flops 1207959552 | bytes 2752512 | tf_op jit(solution)/shard_map/pallas_call | solution.py:142
  13.1 2.9 %collective-permute-start.4 = (bf16[1152,128]{1,0:T(8,128)(2,1)S(1)}, bf16[1152,128]{1,0:T(8,128)(2,1)S(1)}, u32[]{:S(2)}, u32[]{:S(2)}) collective-permute-start(bf16[1152,128]{1,0:T(8,128)(2,1)S(1)} %constant_dynamic-slice_fusion.3), channel_id=1, source_target_pairs={{0,2},{1,5},{2,0},{3,7},{4,6},{5,1},{6,4},{7,3},{8,10},{9,13},{10,... | collective-permute-start | bytes 884744 | tf_op jit(solution)/shard_map/ppermute | solution.py:163
  16.0 0.1 collective-permute-start.9
  16.2 4.6 %collective-permute-done.4 = bf16[1152,128]{1,0:T(8,128)(2,1)S(1)} collective-permute-done((bf16[1152,128]{1,0:T(8,128)(2,1)S(1)}, bf16[1152,128]{1,0:T(8,128)(2,1)S(1)}, u32[]{:S(2)}, u32[]{:S(2)}) %collective-permute-start.4) | collective-permute-done | bytes 294944 | tf_op jit(solution)/shard_map/ppermute | solution.py:163
  20.8 2.2 %collective-permute-start.5 = (bf16[576,128]{1,0:T(8,128)(2,1)S(1)}, bf16[576,128]{1,0:T(8,128)(2,1)S(1)}, u32[]{:S(2)}, u32[]{:S(2)}) collective-permute-start(bf16[576,128]{1,0:T(8,128)(2,1)S(1)} %constant_dynamic-slice_fusion.2), channel_id=1, source_target_pairs={{0,4},{1,3},{2,6},{3,1},{4,0},{5,7},{6,2},{7,5},{8,12},{9,11},{10,... | collective-permute-start | bytes 442376 | tf_op jit(solution)/shard_map/ppermute | solution.py:163
  23.0 1.5 %collective-permute-done.9 = bf16[1152,128]{1,0:T(8,128)(2,1)S(1)} collective-permute-done((bf16[1152,128]{1,0:T(8,128)(2,1)S(1)}, bf16[1152,128]{1,0:T(8,128)(2,1)S(1)}, u32[]{:S(2)}, u32[]{:S(2)}) %collective-permute-start.9) | collective-permute-done | bytes 294944 | tf_op jit(solution)/shard_map/ppermute | solution.py:163
  24.7 2.5 %collective-permute-start.10 = (bf16[576,128]{1,0:T(8,128)(2,1)S(1)}, bf16[576,128]{1,0:T(8,128)(2,1)S(1)}, u32[]{:S(2)}, u32[]{:S(2)}) collective-permute-start(bf16[576,128]{1,0:T(8,128)(2,1)S(1)} %constant_dynamic-slice_fusion), channel_id=1, source_target_pairs={{0,4},{1,3},{2,6},{3,1},{4,0},{5,7},{6,2},{7,5},{8,12},{9,11},{10,... | collective-permute-start | bytes 442376 | tf_op jit(solution)/shard_map/ppermute | solution.py:163
  27.2 2.6 %collective-permute-start.6 = (bf16[576,128]{1,0:T(8,128)(2,1)S(1)}, bf16[576,128]{1,0:T(8,128)(2,1)S(1)}, u32[]{:S(2)}, u32[]{:S(2)}) collective-permute-start(bf16[576,128]{1,0:T(8,128)(2,1)S(1)} %add_convert_fusion.3), channel_id=1, source_target_pairs={{0,8},{1,9},{2,10},{3,11},{4,12},{5,13},{6,14},{7,15},{8,0},{9,1},... | collective-permute-start | bytes 442376 | tf_op jit(solution)/shard_map/ppermute | solution.py:163
  29.9 1.7 %collective-permute-done.10 = bf16[576,128]{1,0:T(8,128)(2,1)S(1)} collective-permute-done((bf16[576,128]{1,0:T(8,128)(2,1)S(1)}, bf16[576,128]{1,0:T(8,128)(2,1)S(1)}, u32[]{:S(2)}, u32[]{:S(2)}) %collective-permute-start.10) | collective-permute-done | bytes 147488 | tf_op jit(solution)/shard_map/ppermute | solution.py:163
  31.6 3.3 %collective-permute-start.11 = (bf16[576,128]{1,0:T(8,128)(2,1)S(1)}, bf16[576,128]{1,0:T(8,128)(2,1)S(1)}, u32[]{:S(2)}, u32[]{:S(2)}) collective-permute-start(bf16[576,128]{1,0:T(8,128)(2,1)S(1)} %add_convert_fusion.2), channel_id=1, source_target_pairs={{0,8},{1,9},{2,10},{3,11},{4,12},{5,13},{6,14},{7,15},{8,0},{9,1},... | collective-permute-start | bytes 442376 | tf_op jit(solution)/shard_map/ppermute | solution.py:163
  35.0 5.7 %collective-permute-done.6 = bf16[576,128]{1,0:T(8,128)(2,1)S(1)} collective-permute-done((bf16[576,128]{1,0:T(8,128)(2,1)S(1)}, bf16[576,128]{1,0:T(8,128)(2,1)S(1)}, u32[]{:S(2)}, u32[]{:S(2)}) %collective-permute-start.6) | collective-permute-done | bytes 147488 | tf_op jit(solution)/shard_map/ppermute | solution.py:163
  40.7 0.1 collective-permute-start.7
  40.8 1.5 %collective-permute-done.11 = bf16[576,128]{1,0:T(8,128)(2,1)S(1)} collective-permute-done((bf16[576,128]{1,0:T(8,128)(2,1)S(1)}, bf16[576,128]{1,0:T(8,128)(2,1)S(1)}, u32[]{:S(2)}, u32[]{:S(2)}) %collective-permute-start.11) | collective-permute-done | bytes 147488 | tf_op jit(solution)/shard_map/ppermute | solution.py:163
  42.4 0.8 %collective-permute-start.12 = (bf16[576,128]{1,0:T(8,128)(2,1)S(1)}, bf16[576,128]{1,0:T(8,128)(2,1)S(1)}, u32[]{:S(2)}, u32[]{:S(2)}) collective-permute-start(bf16[576,128]{1,0:T(8,128)(2,1)S(1)} %multiply_convert_fusion), channel_id=1, source_target_pairs={{0,4},{1,3},{2,6},{3,1},{4,0},{5,7},{6,2},{7,5},{8,12},{9,11},{10,... | collective-permute-start | bytes 442376 | tf_op jit(solution)/shard_map/ppermute | solution.py:163
  43.2 3.3 %collective-permute-done.7 = bf16[576,128]{1,0:T(8,128)(2,1)S(1)} collective-permute-done((bf16[576,128]{1,0:T(8,128)(2,1)S(1)}, bf16[576,128]{1,0:T(8,128)(2,1)S(1)}, u32[]{:S(2)}, u32[]{:S(2)}) %collective-permute-start.7) | collective-permute-done | bytes 147488 | tf_op jit(solution)/shard_map/ppermute | solution.py:163
  46.5 0.1 maximum_select_fusion.2
  46.6 2.5 %collective-permute-start.8 = (bf16[1152,128]{1,0:T(8,128)(2,1)S(1)}, bf16[1152,128]{1,0:T(8,128)(2,1)S(1)}, u32[]{:S(2)}, u32[]{:S(2)}) collective-permute-start(bf16[1152,128]{1,0:T(8,128)(2,1)S(1)} %maximum_select_fusion.2), channel_id=1, source_target_pairs={{0,2},{1,5},{2,0},{3,7},{4,6},{5,1},{6,4},{7,3},{8,10},{9,13},{10,... | collective-permute-start | bytes 884744 | tf_op jit(solution)/shard_map/ppermute | solution.py:163
  49.1 1.8 %shard_map.68 = bf16[512,256]{1,0:T(8,128)(2,1)} custom-call(bf16[512,256]{1,0:T(8,128)(2,1)S(1)} %bitcast.18, bf16[512,256]{1,0:T(8,128)(2,1)S(1)} %get-tuple-element.6.h_ref, bf16[2304,128]{1,0:T(8,128)(2,1)S(1)} %bitcast.11, bf16[2304,128]{1,0:T(8,128)(2,1)S(1)} %collective-permute-done.3.w_other), custom_call_target="tpu_custom_call" | custom-call | flops 603979776 | bytes 1703936 | tf_op jit(solution)/shard_map/pallas_call | solution.py:142
  50.9 0.1 maximum_select_fusion.3
  51.0 1.3 %collective-permute-start.13 = (bf16[1152,128]{1,0:T(8,128)(2,1)S(1)}, bf16[1152,128]{1,0:T(8,128)(2,1)S(1)}, u32[]{:S(2)}, u32[]{:S(2)}) collective-permute-start(bf16[1152,128]{1,0:T(8,128)(2,1)S(1)} %maximum_select_fusion.3), channel_id=1, source_target_pairs={{0,2},{1,5},{2,0},{3,7},{4,6},{5,1},{6,4},{7,3},{8,10},{9,13},{10,... | collective-permute-start | bytes 884744 | tf_op jit(solution)/shard_map/ppermute | solution.py:163
  52.3 1.5 %collective-permute-done.8 = bf16[1152,128]{1,0:T(8,128)(2,1)S(1)} collective-permute-done((bf16[1152,128]{1,0:T(8,128)(2,1)S(1)}, bf16[1152,128]{1,0:T(8,128)(2,1)S(1)}, u32[]{:S(2)}, u32[]{:S(2)}) %collective-permute-start.8) | collective-permute-done | bytes 294944 | tf_op jit(solution)/shard_map/ppermute | solution.py:163
  53.8 1.0 %maximum_select_fusion = bf16[2304,128]{1,0:T(8,128)(2,1)} fusion(bf16[1152,128]{1,0:T(8,128)(2,1)S(1)} %collective-permute-done.8, bf16[1152,128]{1,0:T(8,128)(2,1)S(1)} %maximum_select_fusion.2, pred[]{:T(512)S(6)} %eq.7), kind=kLoop, calls=%fused_computation | loop fusion | flops 2654208 | bytes 1179649 | tf_op jit(solution)/shard_map/jit(_where)/select_n | solution.py:189
  54.8 3.0 %collective-permute-done.13 = bf16[1152,128]{1,0:T(8,128)(2,1)S(1)} collective-permute-done((bf16[1152,128]{1,0:T(8,128)(2,1)S(1)}, bf16[1152,128]{1,0:T(8,128)(2,1)S(1)}, u32[]{:S(2)}, u32[]{:S(2)}) %collective-permute-start.13) | collective-permute-done | bytes 294944 | tf_op jit(solution)/shard_map/ppermute | solution.py:163
  57.8 1.0 %maximum_select_fusion.1 = bf16[2304,128]{1,0:T(8,128)(2,1)} fusion(bf16[1152,128]{1,0:T(8,128)(2,1)S(1)} %collective-permute-done.13, bf16[1152,128]{1,0:T(8,128)(2,1)S(1)} %maximum_select_fusion.3, pred[]{:T(512)S(6)} %eq.7), kind=kLoop, calls=%fused_computation.1 | loop fusion | flops 2654208 | bytes 1179649 | tf_op jit(solution)/shard_map/jit(_where)/select_n | solution.py:189
  (23 shorter events, 0.6 us)
Async XLA Ops:
  0.6 4.0 %collective-permute-start.2 = (bf16[2304,128]{1,0:T(8,128)(2,1)}, bf16[2304,128]{1,0:T(8,128)(2,1)S(1)}, u32[]{:S(2)}, u32[]{:S(2)}) collective-permute-start(bf16[2304,128]{1,0:T(8,128)(2,1)} %bitcast.7), channel_id=1, source_target_pairs={{0,1},{1,0},{2,3},{3,2},{4,5},{5,4},{6,7},{7,6},{8,9},{9,8},{10,11... | collective-permute-start | bytes 1769480 | tf_op jit(solution)/shard_map/ppermute | solution.py:207
  1.1 9.3 %collective-permute-start.3 = (bf16[2304,128]{1,0:T(8,128)(2,1)}, bf16[2304,128]{1,0:T(8,128)(2,1)S(1)}, u32[]{:S(2)}, u32[]{:S(2)}) collective-permute-start(bf16[2304,128]{1,0:T(8,128)(2,1)} %bitcast.9), channel_id=1, source_target_pairs={{0,1},{1,0},{2,3},{3,2},{4,5},{5,4},{6,7},{7,6},{8,9},{9,8},{10,11... | collective-permute-start | bytes 1769480 | tf_op jit(solution)/shard_map/ppermute | solution.py:207
  1.2 3.0 %collective-permute-start = (bf16[512,256]{1,0:T(8,128)(2,1)}, bf16[512,256]{1,0:T(8,128)(2,1)S(1)}, u32[]{:S(2)}, u32[]{:S(2)}) collective-permute-start(bf16[512,256]{1,0:T(8,128)(2,1)} %bitcast.15), channel_id=1, source_target_pairs={{0,1},{1,0},{2,3},{3,2},{4,5},{5,4},{6,7},{7,6},{8,9},{9,8},{10,11... | collective-permute-start | bytes 786440 | tf_op jit(solution)/shard_map/ppermute | solution.py:207
  1.7 2.9 %collective-permute-start.1 = (bf16[512,256]{1,0:T(8,128)(2,1)}, bf16[512,256]{1,0:T(8,128)(2,1)S(1)}, u32[]{:S(2)}, u32[]{:S(2)}) collective-permute-start(bf16[512,256]{1,0:T(8,128)(2,1)} %bitcast.12), channel_id=1, source_target_pairs={{0,1},{1,0},{2,3},{3,2},{4,5},{5,4},{6,7},{7,6},{8,9},{9,8},{10,11... | collective-permute-start | bytes 786440 | tf_op jit(solution)/shard_map/ppermute | solution.py:207
  4.6 1.1 %copy-start = (bf16[9,256,128]{2,1,0:T(8,128)(2,1)S(1)}, bf16[9,256,128]{2,1,0:T(8,128)(2,1)}, u32[]{:S(2)}) copy-start(bf16[9,256,128]{2,1,0:T(8,128)(2,1)} %param.6) | copy-start | bytes 1769476
  5.7 0.9 %copy-start.2 = (bf16[1,16,32,256]{3,2,1,0:T(8,128)(2,1)S(1)}, bf16[1,16,32,256]{3,2,1,0:T(8,128)(2,1)}, u32[]{:S(2)}) copy-start(bf16[1,16,32,256]{3,2,1,0:T(8,128)(2,1)} %param.5) | copy-start | bytes 786436
  6.6 0.9 %copy-start.3 = (bf16[1,16,32,256]{3,2,1,0:T(8,128)(2,1)S(1)}, bf16[1,16,32,256]{3,2,1,0:T(8,128)(2,1)}, u32[]{:S(2)}) copy-start(bf16[1,16,32,256]{3,2,1,0:T(8,128)(2,1)} %param.4) | copy-start | bytes 786436
  7.6 2.9 %copy-start.1 = (bf16[9,256,128]{2,1,0:T(8,128)(2,1)S(1)}, bf16[9,256,128]{2,1,0:T(8,128)(2,1)}, u32[]{:S(2)}) copy-start(bf16[9,256,128]{2,1,0:T(8,128)(2,1)} %param.7) | copy-start | bytes 1769476
  13.1 7.6 %collective-permute-start.4 = (bf16[1152,128]{1,0:T(8,128)(2,1)S(1)}, bf16[1152,128]{1,0:T(8,128)(2,1)S(1)}, u32[]{:S(2)}, u32[]{:S(2)}) collective-permute-start(bf16[1152,128]{1,0:T(8,128)(2,1)S(1)} %constant_dynamic-slice_fusion.3), channel_id=1, source_target_pairs={{0,2},{1,5},{2,0},{3,7},{4,6},{5,1},{6,4},{7,3},{8,10},{9,13},{10,... | collective-permute-start | bytes 884744 | tf_op jit(solution)/shard_map/ppermute | solution.py:163
  16.0 8.5 %collective-permute-start.9 = (bf16[1152,128]{1,0:T(8,128)(2,1)S(1)}, bf16[1152,128]{1,0:T(8,128)(2,1)S(1)}, u32[]{:S(2)}, u32[]{:S(2)}) collective-permute-start(bf16[1152,128]{1,0:T(8,128)(2,1)S(1)} %constant_dynamic-slice_fusion.1), channel_id=1, source_target_pairs={{0,2},{1,5},{2,0},{3,7},{4,6},{5,1},{6,4},{7,3},{8,10},{9,13},{10,... | collective-permute-start | bytes 884744 | tf_op jit(solution)/shard_map/ppermute | solution.py:163
  20.8 6.4 %collective-permute-start.5 = (bf16[576,128]{1,0:T(8,128)(2,1)S(1)}, bf16[576,128]{1,0:T(8,128)(2,1)S(1)}, u32[]{:S(2)}, u32[]{:S(2)}) collective-permute-start(bf16[576,128]{1,0:T(8,128)(2,1)S(1)} %constant_dynamic-slice_fusion.2), channel_id=1, source_target_pairs={{0,4},{1,3},{2,6},{3,1},{4,0},{5,7},{6,2},{7,5},{8,12},{9,11},{10,... | collective-permute-start | bytes 442376 | tf_op jit(solution)/shard_map/ppermute | solution.py:163
  24.7 6.9 %collective-permute-start.10 = (bf16[576,128]{1,0:T(8,128)(2,1)S(1)}, bf16[576,128]{1,0:T(8,128)(2,1)S(1)}, u32[]{:S(2)}, u32[]{:S(2)}) collective-permute-start(bf16[576,128]{1,0:T(8,128)(2,1)S(1)} %constant_dynamic-slice_fusion), channel_id=1, source_target_pairs={{0,4},{1,3},{2,6},{3,1},{4,0},{5,7},{6,2},{7,5},{8,12},{9,11},{10,... | collective-permute-start | bytes 442376 | tf_op jit(solution)/shard_map/ppermute | solution.py:163
  27.2 13.4 %collective-permute-start.6 = (bf16[576,128]{1,0:T(8,128)(2,1)S(1)}, bf16[576,128]{1,0:T(8,128)(2,1)S(1)}, u32[]{:S(2)}, u32[]{:S(2)}) collective-permute-start(bf16[576,128]{1,0:T(8,128)(2,1)S(1)} %add_convert_fusion.3), channel_id=1, source_target_pairs={{0,8},{1,9},{2,10},{3,11},{4,12},{5,13},{6,14},{7,15},{8,0},{9,1},... | collective-permute-start | bytes 442376 | tf_op jit(solution)/shard_map/ppermute | solution.py:163
  31.6 10.7 %collective-permute-start.11 = (bf16[576,128]{1,0:T(8,128)(2,1)S(1)}, bf16[576,128]{1,0:T(8,128)(2,1)S(1)}, u32[]{:S(2)}, u32[]{:S(2)}) collective-permute-start(bf16[576,128]{1,0:T(8,128)(2,1)S(1)} %add_convert_fusion.2), channel_id=1, source_target_pairs={{0,8},{1,9},{2,10},{3,11},{4,12},{5,13},{6,14},{7,15},{8,0},{9,1},... | collective-permute-start | bytes 442376 | tf_op jit(solution)/shard_map/ppermute | solution.py:163
  40.7 8.4 %copy-start.4 = (bf16[1,16,32,256]{3,2,1,0:T(8,128)(2,1)S(1)}, bf16[1,16,32,256]{3,2,1,0:T(8,128)(2,1)}, u32[]{:S(2)}) copy-start(bf16[1,16,32,256]{3,2,1,0:T(8,128)(2,1)} %param.4) | copy-start | bytes 786436
  40.7 5.8 %collective-permute-start.7 = (bf16[576,128]{1,0:T(8,128)(2,1)S(1)}, bf16[576,128]{1,0:T(8,128)(2,1)S(1)}, u32[]{:S(2)}, u32[]{:S(2)}) collective-permute-start(bf16[576,128]{1,0:T(8,128)(2,1)S(1)} %multiply_convert_fusion.1), channel_id=1, source_target_pairs={{0,4},{1,3},{2,6},{3,1},{4,0},{5,7},{6,2},{7,5},{8,12},{9,11},{10,... | collective-permute-start | bytes 442376 | tf_op jit(solution)/shard_map/ppermute | solution.py:163
  42.4 8.5 %collective-permute-start.12 = (bf16[576,128]{1,0:T(8,128)(2,1)S(1)}, bf16[576,128]{1,0:T(8,128)(2,1)S(1)}, u32[]{:S(2)}, u32[]{:S(2)}) collective-permute-start(bf16[576,128]{1,0:T(8,128)(2,1)S(1)} %multiply_convert_fusion), channel_id=1, source_target_pairs={{0,4},{1,3},{2,6},{3,1},{4,0},{5,7},{6,2},{7,5},{8,12},{9,11},{10,... | collective-permute-start | bytes 442376 | tf_op jit(solution)/shard_map/ppermute | solution.py:163
  46.6 7.2 %collective-permute-start.8 = (bf16[1152,128]{1,0:T(8,128)(2,1)S(1)}, bf16[1152,128]{1,0:T(8,128)(2,1)S(1)}, u32[]{:S(2)}, u32[]{:S(2)}) collective-permute-start(bf16[1152,128]{1,0:T(8,128)(2,1)S(1)} %maximum_select_fusion.2), channel_id=1, source_target_pairs={{0,2},{1,5},{2,0},{3,7},{4,6},{5,1},{6,4},{7,3},{8,10},{9,13},{10,... | collective-permute-start | bytes 884744 | tf_op jit(solution)/shard_map/ppermute | solution.py:163
  51.0 6.8 %collective-permute-start.13 = (bf16[1152,128]{1,0:T(8,128)(2,1)S(1)}, bf16[1152,128]{1,0:T(8,128)(2,1)S(1)}, u32[]{:S(2)}, u32[]{:S(2)}) collective-permute-start(bf16[1152,128]{1,0:T(8,128)(2,1)S(1)} %maximum_select_fusion.3), channel_id=1, source_target_pairs={{0,2},{1,5},{2,0},{3,7},{4,6},{5,1},{6,4},{7,3},{8,10},{9,13},{10,... | collective-permute-start | bytes 884744 | tf_op jit(solution)/shard_map/ppermute | solution.py:163

commit v2 on v1

--- a/solution.py
+++ b/solution.py
@@ -9,7 +9,8 @@
 
 F32 = jnp.float32
 BF16 = jnp.bfloat16
-VMEM_LIMIT = 40 * 1024 * 1024
+DEPS = {(1, 2): (2,)}
+VMEM_LIMIT = 16 * 1024 * 1024
 
 
 def column_shifted(field, cols, by):
@@ -45,7 +46,7 @@
 
 
 def first_kernel(
-    cols, x_own, x_other, c_own, c_other, w_own, w_other,
+    cols, x_own, x_other, c_own, c_other, w_own, w_other, ready_ref,
     grad_ref, hidden_ref, slope_ref,
     weight, taps, narrow, turned, pre_ref,
 ):
@@ -74,6 +75,10 @@
     weight_grad(cols, turned, narrow, grad_ref)
 
 
+def ready_kernel(cols, out_ref):
+    out_ref[...] = jnp.zeros(out_ref.shape, F32)
+
+
 def weight_grad(cols, turned, narrow, grad_ref):
     chans = turned.shape[0]
     half = grad_ref.shape[1]
@@ -168,30 +173,73 @@
     return (lax.axis_index("dp") >> jnp.where(core == 0, orders[0][step], orders[1][step])) & 1
 
 
-def summed_over_dp(value, scale):
+def cube_halves(value, orders, step):
+    half = value.shape[0] // 2
+    bit = cube_bit(orders, step)
+    sent = lax.dynamic_slice_in_dim(value, (1 - bit) * half, half, 0)
+    kept = lax.dynamic_slice_in_dim(value, bit * half, half, 0)
+    return sent, kept
+
+
+def added(kept, came):
+    return (kept.astype(F32) + came.astype(F32)).astype(BF16)
+
+
+def after(value, *others):
+    return lax.optimization_barrier((value, *others))[0]
+
+
+def summed_over_dp(early, make_late, scale, outputs):
     devices = lax.axis_size("dp")
     bits = devices.bit_length() - 1
-    if devices != 1 << bits or bits == 0 or value.shape[0] % (1 << (bits - 1)):
-        return (lax.psum(value.astype(F32), "dp") * scale).astype(BF16)
     orders = cube_orders(bits)
-    for step in range(bits - 1):
-        half = value.shape[0] // 2
-        bit = cube_bit(orders, step)
-        sent = lax.dynamic_slice_in_dim(value, (1 - bit) * half, half, 0)
-        kept = lax.dynamic_slice_in_dim(value, bit * half, half, 0)
-        came = cube_swap(sent, orders, step)
-        value = (kept.astype(F32) + came.astype(F32)).astype(BF16)
-    came = cube_swap(value, orders, bits - 1)
-    value = ((value.astype(F32) + came.astype(F32)) * scale).astype(BF16)
-    for step in range(bits - 2, -1, -1):
-        came = cube_swap(value, orders, step)
-        bit = cube_bit(orders, step)
-        value = jnp.where(
-            bit == 0,
-            jnp.concatenate([value, came], 0),
-            jnp.concatenate([came, value], 0),
-        )
-    return value
+    last = bits - 1
+    steps = list(range(bits)) + list(range(bits - 2, -1, -1))
+    values = [early, None]
+    came = [{}, {}]
+
+    def send(which, k):
+        step = steps[k]
+        value = values[which]
+        if k < last:
+            sent, _ = cube_halves(value, orders, step)
+        else:
+            sent = value
+        for other in DEPS.get((which, k), ()):
+            if other == "out":
+                sent = after(sent, outputs)
+            elif other in came[1 - which]:
+                sent = after(sent, came[1 - which][other])
+        came[which][k] = cube_swap(sent, orders, step)
+
+    def take(which, k):
+        step = steps[k]
+        value, got = values[which], came[which][k]
+        if k < last:
+            value = added(cube_halves(value, orders, step)[1], got)
+        elif k == last:
+            value = ((value.astype(F32) + got.astype(F32)) * scale).astype(BF16)
+        else:
+            bit = cube_bit(orders, step)
+            value = jnp.where(
+                bit == 0,
+                jnp.concatenate([value, got], 0),
+                jnp.concatenate([got, value], 0),
+            )
+        values[which] = value
+
+    send(0, 0)
+    values[1] = make_late()
+    for k in range(len(steps)):
+        send(1, k) if k == 0 else None
+        take(0, k)
+        if k + 1 < len(steps):
+            send(0, k + 1)
+        if k >= 1:
+            take(1, k - 1)
+            send(1, k)
+    take(1, len(steps) - 1)
+    return values
 
 
 def body(inputs, cotangent, conv_first, conv_second):
@@ -212,6 +260,7 @@
     narrow = pltpu.VMEM((2, cells + 2 * cols, 3 * half), BF16)
     turned = pltpu.VMEM((chans, 2 * cells), BF16)
     grad_shape = jax.ShapeDtypeStruct((9 * chans, half), BF16)
+    ready = call(ready_kernel, cols, jax.ShapeDtypeStruct((8, 128), F32), [], 4 * unit)
     second, hidden, slope = call(
         first_kernel,
         cols,
@@ -222,16 +271,18 @@
         ),
         [weight, taps, narrow, turned, pltpu.VMEM((cells, chans), F32)],
         3 * unit,
-        x_own, x_other, c_own, c_other, w1_own, w1_other,
-    )
-    first = call(
-        second_kernel,
-        cols,
-        grad_shape,
-        [weight, taps, narrow, turned],
-        2 * unit,
-        x_own, x_other, c_own, c_other, w2_own, w2_other, slope,
-    )
+        x_own, x_other, c_own, c_other, w1_own, w1_other, ready,
+    )
+    def make_late():
+        return call(
+            second_kernel,
+            cols,
+            grad_shape,
+            [weight, taps, narrow, turned],
+            2 * unit,
+            x_own, x_other, c_own, c_other, w2_own, w2_other, slope,
+        )
+
     outputs = call(
         output_kernel,
         cols,
@@ -241,8 +292,7 @@
         x_own, hidden, w2_own, w2_other,
     )
     scale = 1.0 / (inputs.shape[0] * lax.axis_size("dp") * lax.axis_size("shard"))
-    grad_second = summed_over_dp(second, scale)
-    grad_first = summed_over_dp(first, scale)
+    grad_second, grad_first = summed_over_dp(second, make_late, scale, outputs)
     return (
         outputs.reshape(inputs.shape),
         grad_first.reshape(conv_first.shape),

time: 59 us -> 52.2 us (0.88)
  waiting for transfers between devices: 25.7 us -> 17.9 us
  starting transfers between devices: 19.5 us -> 23.6 us
  local copies, waits for them, and re-layouts: 3.06 us -> 0.11 us
    ppermute x10, waiting for transfers between devices: 22.9 us -> 15.9 us  [cube_swap(): return lax.ppermute(value, ('dp', 'shard'), pairs)]
    ppermute x10, starting transfers between devices: 18.4 us -> 22.5 us  [cube_swap(): return lax.ppermute(value, ('dp', 'shard'), pairs)]
    unnamed x10 -> x8, local copies, waits for them, and re-layouts: 2.97 us -> 0.02 us
    ppermute x4, waiting for transfers between devices: 2.85 us -> 2 us  [body(): lax.ppermute(v, 'shard', swap)]
    pallas_call x3 -> x4, Pallas kernels: 7.26 us -> 7.27 us  [call(): pl.pallas_call(functools.partial(kernel, cols), out_shape=outs, in_specs=...]
  transfers between devices with their start and end apart: 14 -> 14, of which waited for: 10 -> 9; matrix products, arithmetic and copies ran while one was open for 3% -> 3% of each run, Pallas kernels for 8% -> 14%
where the time goes in v2:
time: 52.2 us; the launch traced here: 52.1 us
  starting transfers between devices  23.6 us (45%)
  waiting for transfers between devices  17.9 us (34%)
  Pallas kernels  7.27 us (14%)
  other arithmetic  2.48 us (5%)
  between operations  0.74 us (1%)
    ppermute x10, starting transfers between devices, cube_swap(): return lax.ppermute(value, ('dp', 'shard'), pairs)  22.5 us
    ppermute x10, waiting for transfers between devices, cube_swap(): return lax.ppermute(value, ('dp', 'shard'), pairs)  15.9 us
    pallas_call x4, Pallas kernels, call(): pl.pallas_call(functools.partial(kernel, cols), out_shape=outs, in_specs=...  7.27 us
    select_n x4, other arithmetic, take(): jnp.where(bit == 0, jnp.concatenate([value, got], 0), jnp.concatenate([go...  2.13 us
    ppermute x4, waiting for transfers between devices, body(): lax.ppermute(v, 'shard', swap)  2 us
    ppermute x4, starting transfers between devices, body(): lax.ppermute(v, 'shard', swap)  1.11 us
  transfers between devices with their start and end apart: 14, of which 9 were waited for; matrix products, arithmetic and copies ran while one was open for 3% of the time, Pallas kernels for 14%

profile of v2, /device:TPU:0, one launch (start us, length us, event | category | flops | bytes accessed | tf_op | source)
XLA Modules:
  0.0 52.1 jit_solution(3613967373296679894)
XLA Ops:
  0.6 0.5 collective-permute-start.2
  1.1 0.1 collective-permute-start
  1.2 0.4 collective-permute-start.1
  1.7 0.1 collective-permute-start.3
  1.7 1.6 %collective-permute-done.x_other = bf16[512,256]{1,0:T(8,128)(2,1)S(1)} collective-permute-done((bf16[512,256]{1,0:T(8,128)(2,1)}, bf16[512,256]{1,0:T(8,128)(2,1)S(1)}, u32[]{:S(2)}, u32[]{:S(2)}) %collective-permute-start) | collective-permute-done | bytes 262176 | tf_op jit(solution)/shard_map/ppermute | solution.py:255
  3.4 0.4 collective-permute-done.1.c_other
  3.8 2.9 %shard_map.68 = (bf16[2304,128]{1,0:T(8,128)(2,1)S(1)}, bf16[512,256]{1,0:T(8,128)(2,1)S(1)}, f32[1024,128]{1,0:T(8,128)S(1)}) custom-call(bf16[512,256]{1,0:T(8,128)(2,1)S(1)} %bitcast.16, bf16[512,256]{1,0:T(8,128)(2,1)S(1)} %collective-permute-done.x_other, bf16[512,256]{1,0:T(8,128)(2,1)S(1)} %bitcast.13, ...), custom_call_target="tpu_custom_call" | custom-call | flops 1811939328 | bytes 2232320 | tf_op jit(solution)/shard_map/pallas_call | solution.py:147
  6.7 2.9 %collective-permute-start.6 = (bf16[1152,128]{1,0:T(8,128)(2,1)S(1)}, bf16[1152,128]{1,0:T(8,128)(2,1)S(1)}, u32[]{:S(2)}, u32[]{:S(2)}) collective-permute-start(bf16[1152,128]{1,0:T(8,128)(2,1)S(1)} %constant_dynamic-slice_fusion.1), channel_id=1, source_target_pairs={{0,2},{1,5},{2,0},{3,7},{4,6},{5,1},{6,4},{7,3},{8,10},{9,13},{10,... | collective-permute-start | bytes 884744 | tf_op jit(solution)/shard_map/ppermute | solution.py:168
  9.7 2.6 %shard_map.70 = bf16[2304,128]{1,0:T(8,128)(2,1)S(1)} custom-call(bf16[512,256]{1,0:T(8,128)(2,1)S(1)} %bitcast.17, bf16[512,256]{1,0:T(8,128)(2,1)S(1)} %collective-permute-done.x_other, bf16[512,256]{1,0:T(8,128)(2,1)S(1)} %bitcast.14, bf16[512,256]{1,0:T(8,128)(2,1)S(1)} %collective-permute-done.1.c_other, bf16[2304,128]{1,0:T(8,128)(2,1)S(1)} %bitcast.10, ...), custom_call_target="tpu_custom_call" | custom-call | flops 1207959552 | bytes 2752512 | tf_op jit(solution)/shard_map/pallas_call | solution.py:147
  12.3 1.0 %collective-permute-start.4 = (bf16[1152,128]{1,0:T(8,128)(2,1)S(1)}, bf16[1152,128]{1,0:T(8,128)(2,1)S(1)}, u32[]{:S(2)}, u32[]{:S(2)}) collective-permute-start(bf16[1152,128]{1,0:T(8,128)(2,1)S(1)} %constant_dynamic-slice_fusion.3), channel_id=1, source_target_pairs={{0,2},{1,5},{2,0},{3,7},{4,6},{5,1},{6,4},{7,3},{8,10},{9,13},{10,... | collective-permute-start | bytes 884744 | tf_op jit(solution)/shard_map/ppermute | solution.py:168
  13.3 1.1 %collective-permute-done.6 = bf16[1152,128]{1,0:T(8,128)(2,1)S(1)} collective-permute-done((bf16[1152,128]{1,0:T(8,128)(2,1)S(1)}, bf16[1152,128]{1,0:T(8,128)(2,1)S(1)}, u32[]{:S(2)}, u32[]{:S(2)}) %collective-permute-start.6) | collective-permute-done | bytes 294944 | tf_op jit(solution)/shard_map/ppermute | solution.py:168
  14.4 0.1 add_convert_fusion
  14.5 2.2 %collective-permute-start.7 = (bf16[576,128]{1,0:T(8,128)(2,1)S(1)}, bf16[576,128]{1,0:T(8,128)(2,1)S(1)}, u32[]{:S(2)}, u32[]{:S(2)}) collective-permute-start(bf16[576,128]{1,0:T(8,128)(2,1)S(1)} %constant_dynamic-slice_fusion), channel_id=1, source_target_pairs={{0,4},{1,3},{2,6},{3,1},{4,0},{5,7},{6,2},{7,5},{8,12},{9,11},{10,... | collective-permute-start | bytes 442376 | tf_op jit(solution)/shard_map/ppermute | solution.py:168
  16.7 4.0 %collective-permute-done.4 = bf16[1152,128]{1,0:T(8,128)(2,1)S(1)} collective-permute-done((bf16[1152,128]{1,0:T(8,128)(2,1)S(1)}, bf16[1152,128]{1,0:T(8,128)(2,1)S(1)}, u32[]{:S(2)}, u32[]{:S(2)}) %collective-permute-start.4) | collective-permute-done | bytes 294944 | tf_op jit(solution)/shard_map/ppermute | solution.py:168
  20.6 0.1 add_convert_fusion.1
  20.8 1.6 %collective-permute-start.5 = (bf16[576,128]{1,0:T(8,128)(2,1)S(1)}, bf16[576,128]{1,0:T(8,128)(2,1)S(1)}, u32[]{:S(2)}, u32[]{:S(2)}) collective-permute-start(bf16[576,128]{1,0:T(8,128)(2,1)S(1)} %constant_dynamic-slice_fusion.2), channel_id=1, source_target_pairs={{0,4},{1,3},{2,6},{3,1},{4,0},{5,7},{6,2},{7,5},{8,12},{9,11},{10,... | collective-permute-start | bytes 442376 | tf_op jit(solution)/shard_map/ppermute | solution.py:168
  22.4 2.7 %collective-permute-start.8 = (bf16[576,128]{1,0:T(8,128)(2,1)S(1)}, bf16[576,128]{1,0:T(8,128)(2,1)S(1)}, u32[]{:S(2)}, u32[]{:S(2)}) collective-permute-start(bf16[576,128]{1,0:T(8,128)(2,1)S(1)} %add_convert_fusion.2), channel_id=1, source_target_pairs={{0,8},{1,9},{2,10},{3,11},{4,12},{5,13},{6,14},{7,15},{8,0},{9,1},... | collective-permute-start | bytes 442376 | tf_op jit(solution)/shard_map/ppermute | solution.py:168
  25.1 1.4 %collective-permute-done.5 = bf16[576,128]{1,0:T(8,128)(2,1)S(1)} collective-permute-done((bf16[576,128]{1,0:T(8,128)(2,1)S(1)}, bf16[576,128]{1,0:T(8,128)(2,1)S(1)}, u32[]{:S(2)}, u32[]{:S(2)}) %collective-permute-start.5) | collective-permute-done | bytes 147488 | tf_op jit(solution)/shard_map/ppermute | solution.py:168
  26.6 3.6 %collective-permute-done.8 = bf16[576,128]{1,0:T(8,128)(2,1)S(1)} collective-permute-done((bf16[576,128]{1,0:T(8,128)(2,1)S(1)}, bf16[576,128]{1,0:T(8,128)(2,1)S(1)}, u32[]{:S(2)}, u32[]{:S(2)}) %collective-permute-start.8) | collective-permute-done | bytes 147488 | tf_op jit(solution)/shard_map/ppermute | solution.py:168
  30.1 1.0 %collective-permute-start.9 = (bf16[576,128]{1,0:T(8,128)(2,1)S(1)}, bf16[576,128]{1,0:T(8,128)(2,1)S(1)}, u32[]{:S(2)}, u32[]{:S(2)}) collective-permute-start(bf16[576,128]{1,0:T(8,128)(2,1)S(1)} %add_convert_fusion.3), channel_id=1, source_target_pairs={{0,8},{1,9},{2,10},{3,11},{4,12},{5,13},{6,14},{7,15},{8,0},{9,1},... | collective-permute-start | bytes 442376 | tf_op jit(solution)/shard_map/ppermute | solution.py:168
  31.2 4.7 %collective-permute-start.12 = (bf16[576,128]{1,0:T(8,128)(2,1)S(1)}, bf16[576,128]{1,0:T(8,128)(2,1)S(1)}, u32[]{:S(2)}, u32[]{:S(2)}) collective-permute-start(bf16[576,128]{1,0:T(8,128)(2,1)S(1)} %multiply_convert_fusion), channel_id=1, source_target_pairs={{0,4},{1,3},{2,6},{3,1},{4,0},{5,7},{6,2},{7,5},{8,12},{9,11},{10,... | collective-permute-start | bytes 442376 | tf_op jit(solution)/shard_map/ppermute | solution.py:168
  35.9 0.9 %collective-permute-done.9 = bf16[576,128]{1,0:T(8,128)(2,1)S(1)} collective-permute-done((bf16[576,128]{1,0:T(8,128)(2,1)S(1)}, bf16[576,128]{1,0:T(8,128)(2,1)S(1)}, u32[]{:S(2)}, u32[]{:S(2)}) %collective-permute-start.9) | collective-permute-done | bytes 147488 | tf_op jit(solution)/shard_map/ppermute | solution.py:168
  36.9 2.2 %collective-permute-start.10 = (bf16[576,128]{1,0:T(8,128)(2,1)S(1)}, bf16[576,128]{1,0:T(8,128)(2,1)S(1)}, u32[]{:S(2)}, u32[]{:S(2)}) collective-permute-start(bf16[576,128]{1,0:T(8,128)(2,1)S(1)} %multiply_convert_fusion.1), channel_id=1, source_target_pairs={{0,4},{1,3},{2,6},{3,1},{4,0},{5,7},{6,2},{7,5},{8,12},{9,11},{10,... | collective-permute-start | bytes 442376 | tf_op jit(solution)/shard_map/ppermute | solution.py:168
  39.1 0.1 maximum_select_fusion.3
  39.2 1.5 %collective-permute-start.13 = (bf16[1152,128]{1,0:T(8,128)(2,1)S(1)}, bf16[1152,128]{1,0:T(8,128)(2,1)S(1)}, u32[]{:S(2)}, u32[]{:S(2)}) collective-permute-start(bf16[1152,128]{1,0:T(8,128)(2,1)S(1)} %maximum_select_fusion.3), channel_id=1, source_target_pairs={{0,2},{1,5},{2,0},{3,7},{4,6},{5,1},{6,4},{7,3},{8,10},{9,13},{10,... | collective-permute-start | bytes 884744 | tf_op jit(solution)/shard_map/ppermute | solution.py:168
  40.6 1.8 %shard_map.69 = bf16[512,256]{1,0:T(8,128)(2,1)} custom-call(bf16[512,256]{1,0:T(8,128)(2,1)S(1)} %bitcast.18, bf16[512,256]{1,0:T(8,128)(2,1)S(1)} %get-tuple-element.7.h_ref, bf16[2304,128]{1,0:T(8,128)(2,1)S(1)} %bitcast.11, bf16[2304,128]{1,0:T(8,128)(2,1)S(1)} %collective-permute-done.3.w_other), custom_call_target="tpu_custom_call" | custom-call | flops 603979776 | bytes 1703936 | tf_op jit(solution)/shard_map/pallas_call | solution.py:147
  42.4 1.2 %collective-permute-done.10 = bf16[576,128]{1,0:T(8,128)(2,1)S(1)} collective-permute-done((bf16[576,128]{1,0:T(8,128)(2,1)S(1)}, bf16[576,128]{1,0:T(8,128)(2,1)S(1)}, u32[]{:S(2)}, u32[]{:S(2)}) %collective-permute-start.10) | collective-permute-done | bytes 147488 | tf_op jit(solution)/shard_map/ppermute | solution.py:168
  43.6 0.1 maximum_select_fusion.2
  43.7 2.7 %collective-permute-start.11 = (bf16[1152,128]{1,0:T(8,128)(2,1)S(1)}, bf16[1152,128]{1,0:T(8,128)(2,1)S(1)}, u32[]{:S(2)}, u32[]{:S(2)}) collective-permute-start(bf16[1152,128]{1,0:T(8,128)(2,1)S(1)} %maximum_select_fusion.2), channel_id=1, source_target_pairs={{0,2},{1,5},{2,0},{3,7},{4,6},{5,1},{6,4},{7,3},{8,10},{9,13},{10,... | collective-permute-start | bytes 884744 | tf_op jit(solution)/shard_map/ppermute | solution.py:168
  46.4 1.0 %maximum_select_fusion.1 = bf16[2304,128]{1,0:T(8,128)(2,1)} fusion(bf16[1152,128]{1,0:T(8,128)(2,1)S(1)} %collective-permute-done.13, bf16[1152,128]{1,0:T(8,128)(2,1)S(1)} %maximum_select_fusion.3, pred[]{:T(512)S(6)} %eq.7), kind=kLoop, calls=%fused_computation.1 | loop fusion | flops 2654208 | bytes 1179649 | tf_op jit(solution)/shard_map/jit(_where)/select_n | solution.py:224
  47.4 3.7 %collective-permute-done.11 = bf16[1152,128]{1,0:T(8,128)(2,1)S(1)} collective-permute-done((bf16[1152,128]{1,0:T(8,128)(2,1)S(1)}, bf16[1152,128]{1,0:T(8,128)(2,1)S(1)}, u32[]{:S(2)}, u32[]{:S(2)}) %collective-permute-start.11) | collective-permute-done | bytes 294944 | tf_op jit(solution)/shard_map/ppermute | solution.py:168
  51.1 1.0 %maximum_select_fusion = bf16[2304,128]{1,0:T(8,128)(2,1)} fusion(bf16[1152,128]{1,0:T(8,128)(2,1)S(1)} %collective-permute-done.11, bf16[1152,128]{1,0:T(8,128)(2,1)S(1)} %maximum_select_fusion.2, pred[]{:T(512)S(6)} %eq.7), kind=kLoop, calls=%fused_computation | loop fusion | flops 2654208 | bytes 1179649 | tf_op jit(solution)/shard_map/jit(_where)/select_n | solution.py:224
  (22 shorter events, 0.3 us)
Async XLA Ops:
  0.6 3.1 %collective-permute-start.2 = (bf16[2304,128]{1,0:T(8,128)(2,1)}, bf16[2304,128]{1,0:T(8,128)(2,1)S(1)}, u32[]{:S(2)}, u32[]{:S(2)}) collective-permute-start(bf16[2304,128]{1,0:T(8,128)(2,1)} %bitcast.7), channel_id=1, source_target_pairs={{0,1},{1,0},{2,3},{3,2},{4,5},{5,4},{6,7},{7,6},{8,9},{9,8},{10,11... | collective-permute-start | bytes 1769480 | tf_op jit(solution)/shard_map/ppermute | solution.py:255
  1.1 2.2 %collective-permute-start = (bf16[512,256]{1,0:T(8,128)(2,1)}, bf16[512,256]{1,0:T(8,128)(2,1)S(1)}, u32[]{:S(2)}, u32[]{:S(2)}) collective-permute-start(bf16[512,256]{1,0:T(8,128)(2,1)} %bitcast.15), channel_id=1, source_target_pairs={{0,1},{1,0},{2,3},{3,2},{4,5},{5,4},{6,7},{7,6},{8,9},{9,8},{10,11... | collective-permute-start | bytes 786440 | tf_op jit(solution)/shard_map/ppermute | solution.py:255
  1.2 2.5 %collective-permute-start.1 = (bf16[512,256]{1,0:T(8,128)(2,1)}, bf16[512,256]{1,0:T(8,128)(2,1)S(1)}, u32[]{:S(2)}, u32[]{:S(2)}) collective-permute-start(bf16[512,256]{1,0:T(8,128)(2,1)} %bitcast.12), channel_id=1, source_target_pairs={{0,1},{1,0},{2,3},{3,2},{4,5},{5,4},{6,7},{7,6},{8,9},{9,8},{10,11... | collective-permute-start | bytes 786440 | tf_op jit(solution)/shard_map/ppermute | solution.py:255
  1.7 8.0 %collective-permute-start.3 = (bf16[2304,128]{1,0:T(8,128)(2,1)}, bf16[2304,128]{1,0:T(8,128)(2,1)S(1)}, u32[]{:S(2)}, u32[]{:S(2)}) collective-permute-start(bf16[2304,128]{1,0:T(8,128)(2,1)} %bitcast.9), channel_id=1, source_target_pairs={{0,1},{1,0},{2,3},{3,2},{4,5},{5,4},{6,7},{7,6},{8,9},{9,8},{10,11... | collective-permute-start | bytes 1769480 | tf_op jit(solution)/shard_map/ppermute | solution.py:255
  1.7 2.0 %copy-start = (bf16[9,256,128]{2,1,0:T(8,128)(2,1)S(1)}, bf16[9,256,128]{2,1,0:T(8,128)(2,1)}, u32[]{:S(2)}) copy-start(bf16[9,256,128]{2,1,0:T(8,128)(2,1)} %param.6) | copy-start | bytes 1769476
  1.7 2.0 %copy-start.2 = (bf16[1,16,32,256]{3,2,1,0:T(8,128)(2,1)S(1)}, bf16[1,16,32,256]{3,2,1,0:T(8,128)(2,1)}, u32[]{:S(2)}) copy-start(bf16[1,16,32,256]{3,2,1,0:T(8,128)(2,1)} %param.5) | copy-start | bytes 786436
  1.7 2.0 %copy-start.3 = (bf16[1,16,32,256]{3,2,1,0:T(8,128)(2,1)S(1)}, bf16[1,16,32,256]{3,2,1,0:T(8,128)(2,1)}, u32[]{:S(2)}) copy-start(bf16[1,16,32,256]{3,2,1,0:T(8,128)(2,1)} %param.4) | copy-start | bytes 786436
  6.7 3.0 %copy-start.1 = (bf16[9,256,128]{2,1,0:T(8,128)(2,1)S(1)}, bf16[9,256,128]{2,1,0:T(8,128)(2,1)}, u32[]{:S(2)}) copy-start(bf16[9,256,128]{2,1,0:T(8,128)(2,1)} %param.7) | copy-start | bytes 1769476
  6.7 7.6 %collective-permute-start.6 = (bf16[1152,128]{1,0:T(8,128)(2,1)S(1)}, bf16[1152,128]{1,0:T(8,128)(2,1)S(1)}, u32[]{:S(2)}, u32[]{:S(2)}) collective-permute-start(bf16[1152,128]{1,0:T(8,128)(2,1)S(1)} %constant_dynamic-slice_fusion.1), channel_id=1, source_target_pairs={{0,2},{1,5},{2,0},{3,7},{4,6},{5,1},{6,4},{7,3},{8,10},{9,13},{10,... | collective-permute-start | bytes 884744 | tf_op jit(solution)/shard_map/ppermute | solution.py:168
  12.3 8.4 %collective-permute-start.4 = (bf16[1152,128]{1,0:T(8,128)(2,1)S(1)}, bf16[1152,128]{1,0:T(8,128)(2,1)S(1)}, u32[]{:S(2)}, u32[]{:S(2)}) collective-permute-start(bf16[1152,128]{1,0:T(8,128)(2,1)S(1)} %constant_dynamic-slice_fusion.3), channel_id=1, source_target_pairs={{0,2},{1,5},{2,0},{3,7},{4,6},{5,1},{6,4},{7,3},{8,10},{9,13},{10,... | collective-permute-start | bytes 884744 | tf_op jit(solution)/shard_map/ppermute | solution.py:168
  14.5 7.9 %collective-permute-start.7 = (bf16[576,128]{1,0:T(8,128)(2,1)S(1)}, bf16[576,128]{1,0:T(8,128)(2,1)S(1)}, u32[]{:S(2)}, u32[]{:S(2)}) collective-permute-start(bf16[576,128]{1,0:T(8,128)(2,1)S(1)} %constant_dynamic-slice_fusion), channel_id=1, source_target_pairs={{0,4},{1,3},{2,6},{3,1},{4,0},{5,7},{6,2},{7,5},{8,12},{9,11},{10,... | collective-permute-start | bytes 442376 | tf_op jit(solution)/shard_map/ppermute | solution.py:168
  20.8 5.8 %collective-permute-start.5 = (bf16[576,128]{1,0:T(8,128)(2,1)S(1)}, bf16[576,128]{1,0:T(8,128)(2,1)S(1)}, u32[]{:S(2)}, u32[]{:S(2)}) collective-permute-start(bf16[576,128]{1,0:T(8,128)(2,1)S(1)} %constant_dynamic-slice_fusion.2), channel_id=1, source_target_pairs={{0,4},{1,3},{2,6},{3,1},{4,0},{5,7},{6,2},{7,5},{8,12},{9,11},{10,... | collective-permute-start | bytes 442376 | tf_op jit(solution)/shard_map/ppermute | solution.py:168
  22.4 7.7 %collective-permute-start.8 = (bf16[576,128]{1,0:T(8,128)(2,1)S(1)}, bf16[576,128]{1,0:T(8,128)(2,1)S(1)}, u32[]{:S(2)}, u32[]{:S(2)}) collective-permute-start(bf16[576,128]{1,0:T(8,128)(2,1)S(1)} %add_convert_fusion.2), channel_id=1, source_target_pairs={{0,8},{1,9},{2,10},{3,11},{4,12},{5,13},{6,14},{7,15},{8,0},{9,1},... | collective-permute-start | bytes 442376 | tf_op jit(solution)/shard_map/ppermute | solution.py:168
  30.1 6.7 %collective-permute-start.9 = (bf16[576,128]{1,0:T(8,128)(2,1)S(1)}, bf16[576,128]{1,0:T(8,128)(2,1)S(1)}, u32[]{:S(2)}, u32[]{:S(2)}) collective-permute-start(bf16[576,128]{1,0:T(8,128)(2,1)S(1)} %add_convert_fusion.3), channel_id=1, source_target_pairs={{0,8},{1,9},{2,10},{3,11},{4,12},{5,13},{6,14},{7,15},{8,0},{9,1},... | collective-permute-start | bytes 442376 | tf_op jit(solution)/shard_map/ppermute | solution.py:168
  31.2 7.9 %collective-permute-start.12 = (bf16[576,128]{1,0:T(8,128)(2,1)S(1)}, bf16[576,128]{1,0:T(8,128)(2,1)S(1)}, u32[]{:S(2)}, u32[]{:S(2)}) collective-permute-start(bf16[576,128]{1,0:T(8,128)(2,1)S(1)} %multiply_convert_fusion), channel_id=1, source_target_pairs={{0,4},{1,3},{2,6},{3,1},{4,0},{5,7},{6,2},{7,5},{8,12},{9,11},{10,... | collective-permute-start | bytes 442376 | tf_op jit(solution)/shard_map/ppermute | solution.py:168
  36.9 6.7 %collective-permute-start.10 = (bf16[576,128]{1,0:T(8,128)(2,1)S(1)}, bf16[576,128]{1,0:T(8,128)(2,1)S(1)}, u32[]{:S(2)}, u32[]{:S(2)}) collective-permute-start(bf16[576,128]{1,0:T(8,128)(2,1)S(1)} %multiply_convert_fusion.1), channel_id=1, source_target_pairs={{0,4},{1,3},{2,6},{3,1},{4,0},{5,7},{6,2},{7,5},{8,12},{9,11},{10,... | collective-permute-start | bytes 442376 | tf_op jit(solution)/shard_map/ppermute | solution.py:168
  39.2 7.2 %collective-permute-start.13 = (bf16[1152,128]{1,0:T(8,128)(2,1)S(1)}, bf16[1152,128]{1,0:T(8,128)(2,1)S(1)}, u32[]{:S(2)}, u32[]{:S(2)}) collective-permute-start(bf16[1152,128]{1,0:T(8,128)(2,1)S(1)} %maximum_select_fusion.3), channel_id=1, source_target_pairs={{0,2},{1,5},{2,0},{3,7},{4,6},{5,1},{6,4},{7,3},{8,10},{9,13},{10,... | collective-permute-start | bytes 884744 | tf_op jit(solution)/shard_map/ppermute | solution.py:168
  43.7 7.4 %collective-permute-start.11 = (bf16[1152,128]{1,0:T(8,128)(2,1)S(1)}, bf16[1152,128]{1,0:T(8,128)(2,1)S(1)}, u32[]{:S(2)}, u32[]{:S(2)}) collective-permute-start(bf16[1152,128]{1,0:T(8,128)(2,1)S(1)} %maximum_select_fusion.2), channel_id=1, source_target_pairs={{0,2},{1,5},{2,0},{3,7},{4,6},{5,1},{6,4},{7,3},{8,10},{9,13},{10,... | collective-permute-start | bytes 884744 | tf_op jit(solution)/shard_map/ppermute | solution.py:168

commit v3 on v1

--- a/solution.py
+++ b/solution.py
@@ -9,7 +9,7 @@
 
 F32 = jnp.float32
 BF16 = jnp.bfloat16
-VMEM_LIMIT = 40 * 1024 * 1024
+VMEM_LIMIT = 16 * 1024 * 1024
 
 
 def column_shifted(field, cols, by):
@@ -45,7 +45,7 @@
 
 
 def first_kernel(
-    cols, x_own, x_other, c_own, c_other, w_own, w_other,
+    cols, x_own, x_other, c_own, c_other, w_own, w_other, ready_ref,
     grad_ref, hidden_ref, slope_ref,
     weight, taps, narrow, turned, pre_ref,
 ):
@@ -74,6 +74,10 @@
     weight_grad(cols, turned, narrow, grad_ref)
 
 
+def ready_kernel(cols, out_ref):
+    out_ref[...] = jnp.zeros(out_ref.shape, F32)
+
+
 def weight_grad(cols, turned, narrow, grad_ref):
     chans = turned.shape[0]
     half = grad_ref.shape[1]
@@ -150,48 +154,61 @@
     )(*args)
 
 
-def cube_orders(bits):
-    plain = list(range(bits))
-    return plain, ([1, 0] + plain[2:] if bits > 2 else plain)
-
-
-def cube_swap(value, orders, step):
-    devices = lax.axis_size("dp")
-    pairs = [
-        (2 * d + c, 2 * (d ^ (1 << orders[c][step])) + c) for d in range(devices) for c in range(2)
-    ]
-    return lax.ppermute(value, ("dp", "shard"), pairs)
-
-
-def cube_bit(orders, step):
-    core = lax.axis_index("shard")
-    return (lax.axis_index("dp") >> jnp.where(core == 0, orders[0][step], orders[1][step])) & 1
-
-
-def summed_over_dp(value, scale):
-    devices = lax.axis_size("dp")
-    bits = devices.bit_length() - 1
-    if devices != 1 << bits or bits == 0 or value.shape[0] % (1 << (bits - 1)):
-        return (lax.psum(value.astype(F32), "dp") * scale).astype(BF16)
-    orders = cube_orders(bits)
-    for step in range(bits - 1):
-        half = value.shape[0] // 2
-        bit = cube_bit(orders, step)
-        sent = lax.dynamic_slice_in_dim(value, (1 - bit) * half, half, 0)
-        kept = lax.dynamic_slice_in_dim(value, bit * half, half, 0)
-        came = cube_swap(sent, orders, step)
-        value = (kept.astype(F32) + came.astype(F32)).astype(BF16)
-    came = cube_swap(value, orders, bits - 1)
-    value = ((value.astype(F32) + came.astype(F32)) * scale).astype(BF16)
-    for step in range(bits - 2, -1, -1):
-        came = cube_swap(value, orders, step)
-        bit = cube_bit(orders, step)
-        value = jnp.where(
-            bit == 0,
-            jnp.concatenate([value, came], 0),
-            jnp.concatenate([came, value], 0),
-        )
-    return value
+def swapped(value, mask):
+    pairs = [(d, d ^ mask) for d in range(lax.axis_size("dp"))]
+    return lax.ppermute(value, "dp", pairs)
+
+
+def after(value, *others):
+    return lax.optimization_barrier((value, *others))[0]
+
+
+class Summed:
+    def __init__(self, value, scale):
+        devices = lax.axis_size("dp")
+        bits = devices.bit_length() - 1
+        assert devices == 1 << bits
+        self.near = min(4, devices)
+        self.far = [1 << k for k in range(self.near.bit_length() - 1, bits)]
+        self.rows = value.shape[0] // self.near
+        self.value, self.scale = value, scale
+        self.at = lax.axis_index("dp") % self.near
+
+    def quarter(self, index):
+        return lax.dynamic_slice_in_dim(self.value, index * self.rows, self.rows, 0)
+
+    def scatter(self):
+        sent = [self.quarter(self.at ^ mask) for mask in range(1, self.near)]
+        self.came = [swapped(v, mask + 1) for mask, v in enumerate(sent)]
+
+    def add(self):
+        total = self.quarter(self.at).astype(F32)
+        for came in self.came:
+            total = total + came.astype(F32)
+        self.sum = total if not self.far else total.astype(BF16)
+
+    def swap(self, *others):
+        for k, mask in enumerate(self.far):
+            sent = after(self.sum, *others) if k == 0 and others else self.sum
+            self.came = [swapped(sent, mask)]
+            if k + 1 < len(self.far):
+                self.sum = (self.sum.astype(F32) + self.came[0].astype(F32)).astype(BF16)
+
+    def finish(self):
+        total = self.sum.astype(F32)
+        if self.far:
+            total = total + self.came[0].astype(F32)
+        self.sum = (total * self.scale).astype(BF16)
+
+    def gather(self, *others):
+        sent = after(self.sum, *others) if others else self.sum
+        self.came = [swapped(sent, mask) for mask in range(1, self.near)]
+
+    def result(self):
+        whole = jnp.zeros(self.value.shape, BF16)
+        for mask, piece in enumerate([self.sum] + self.came):
+            whole = lax.dynamic_update_slice_in_dim(whole, piece, (self.at ^ mask) * self.rows, 0)
+        return whole
 
 
 def body(inputs, cotangent, conv_first, conv_second):
@@ -212,6 +229,7 @@
     narrow = pltpu.VMEM((2, cells + 2 * cols, 3 * half), BF16)
     turned = pltpu.VMEM((chans, 2 * cells), BF16)
     grad_shape = jax.ShapeDtypeStruct((9 * chans, half), BF16)
+    ready = call(ready_kernel, cols, jax.ShapeDtypeStruct((8, 128), F32), [], 4 * unit)
     second, hidden, slope = call(
         first_kernel,
         cols,
@@ -222,16 +240,18 @@
         ),
         [weight, taps, narrow, turned, pltpu.VMEM((cells, chans), F32)],
         3 * unit,
-        x_own, x_other, c_own, c_other, w1_own, w1_other,
-    )
-    first = call(
-        second_kernel,
-        cols,
-        grad_shape,
-        [weight, taps, narrow, turned],
-        2 * unit,
-        x_own, x_other, c_own, c_other, w2_own, w2_other, slope,
-    )
+        x_own, x_other, c_own, c_other, w1_own, w1_other, ready,
+    )
+    def make_late():
+        return call(
+            second_kernel,
+            cols,
+            grad_shape,
+            [weight, taps, narrow, turned],
+            2 * unit,
+            x_own, x_other, c_own, c_other, w2_own, w2_other, slope,
+        )
+
     outputs = call(
         output_kernel,
         cols,
@@ -241,8 +261,19 @@
         x_own, hidden, w2_own, w2_other,
     )
     scale = 1.0 / (inputs.shape[0] * lax.axis_size("dp") * lax.axis_size("shard"))
-    grad_second = summed_over_dp(second, scale)
-    grad_first = summed_over_dp(first, scale)
+    early, late = Summed(second, scale), None
+    early.scatter()
+    late = Summed(make_late(), scale)
+    late.scatter()
+    early.add()
+    early.swap()
+    late.add()
+    late.swap()
+    early.finish()
+    early.gather()
+    late.finish()
+    late.gather()
+    grad_second, grad_first = early.result(), late.result()
     return (
         outputs.reshape(inputs.shape),
         grad_first.reshape(conv_first.shape),

time: 59 us -> 49.9 us (0.85)
  waiting for transfers between devices: 25.7 us -> 17.8 us
  starting transfers between devices: 19.5 us -> 22.3 us
  other arithmetic: 2.48 us -> 0.34 us
  local copies, waits for them, and re-layouts: 3.06 us -> 1.19 us
    ppermute x10 -> x14, waiting for transfers between devices: 22.9 us -> 15 us  [swapped(): return lax.ppermute(value, 'dp', pairs)]
    ppermute x10 -> x14, starting transfers between devices: 18.4 us -> 21.2 us  [swapped(): return lax.ppermute(value, 'dp', pairs)]
    unnamed x10 -> x12, local copies, waits for them, and re-layouts: 2.97 us -> 0.82 us
    select_n x4 -> x0, other arithmetic: 2.13 us -> none  [summed_over_dp(): jnp.where(bit == 0, jnp.concatenate([value, came], 0), jnp.concatenate([c...]
    pallas_call x3 -> x4, Pallas kernels: 7.26 us -> 7.29 us  [call(): pl.pallas_call(functools.partial(kernel, cols), out_shape=outs, in_specs=...]
  transfers between devices with their start and end apart: 14 -> 18, of which waited for: 10 -> 9; matrix products, arithmetic and copies ran while one was open for 3% -> 1% of each run, Pallas kernels for 8% -> 15%
where the time goes in v3:
time: 49.9 us; the launch traced here: 49.7 us
  starting transfers between devices  22.3 us (45%)
  waiting for transfers between devices  17.8 us (36%)
  Pallas kernels  7.29 us (15%)
  local copies, waits for them, and re-layouts  1.19 us (2%)
  between operations  0.78 us (2%)
    ppermute x14, starting transfers between devices, swapped(): return lax.ppermute(value, 'dp', pairs)  21.2 us
    ppermute x14, waiting for transfers between devices, swapped(): return lax.ppermute(value, 'dp', pairs)  15 us
    pallas_call x4, Pallas kernels, call(): pl.pallas_call(functools.partial(kernel, cols), out_shape=outs, in_specs=...  7.29 us
    ppermute x4, waiting for transfers between devices, body(): lax.ppermute(v, 'shard', swap)  2.84 us
    ppermute x4, starting transfers between devices, body(): lax.ppermute(v, 'shard', swap)  1.11 us
  transfers between devices with their start and end apart: 18, of which 9 were waited for; matrix products, arithmetic and copies ran while one was open for 1% of the time, Pallas kernels for 15%

profile of v3, /device:TPU:0, one launch (start us, length us, event | category | flops | bytes accessed | tf_op | source)
XLA Modules:
  0.0 49.7 jit_solution(13900146757284432181)
XLA Ops:
  0.6 0.5 %collective-permute-start.2 = (bf16[2304,128]{1,0:T(8,128)(2,1)}, bf16[2304,128]{1,0:T(8,128)(2,1)S(1)}, u32[]{:S(2)}, u32[]{:S(2)}) collective-permute-start(bf16[2304,128]{1,0:T(8,128)(2,1)} %bitcast.7), channel_id=1, source_target_pairs={{0,1},{1,0},{2,3},{3,2},{4,5},{5,4},{6,7},{7,6},{8,9},{9,8},{10,11... | collective-permute-start | bytes 1769480 | tf_op jit(solution)/shard_map/ppermute | solution.py:224
  1.2 0.4 collective-permute-start
  1.7 0.1 collective-permute-start.1
  1.7 2.5 %collective-permute-done.x_other = bf16[512,256]{1,0:T(8,128)(2,1)S(1)} collective-permute-done((bf16[512,256]{1,0:T(8,128)(2,1)}, bf16[512,256]{1,0:T(8,128)(2,1)S(1)}, u32[]{:S(2)}, u32[]{:S(2)}) %collective-permute-start) | collective-permute-done | bytes 262176 | tf_op jit(solution)/shard_map/ppermute | solution.py:224
  4.2 0.4 collective-permute-done.1.c_other
  4.6 2.9 %shard_map.68 = (bf16[2304,128]{1,0:T(8,128)(2,1)S(1)}, bf16[512,256]{1,0:T(8,128)(2,1)S(1)}, f32[1024,128]{1,0:T(8,128)S(1)}) custom-call(bf16[512,256]{1,0:T(8,128)(2,1)S(1)} %bitcast.16, bf16[512,256]{1,0:T(8,128)(2,1)S(1)} %collective-permute-done.x_other, bf16[512,256]{1,0:T(8,128)(2,1)S(1)} %bitcast.13, ...), custom_call_target="tpu_custom_call" | custom-call | flops 1811939328 | bytes 2232320 | tf_op jit(solution)/shard_map/pallas_call | solution.py:146
  7.6 2.9 %collective-permute-start.11 = (bf16[576,128]{1,0:T(8,128)(2,1)S(1)}, bf16[576,128]{1,0:T(8,128)(2,1)S(1)}, u32[]{:S(2)}, u32[]{:S(2)}) collective-permute-start(bf16[576,128]{1,0:T(8,128)(2,1)S(1)} %get-tuple-element.13), channel_id=1, source_target_pairs={{0,2},{2,0},{4,6},{6,4},{8,10},{10,8},{12,14},{14,12},{1,3},{3,1},... | collective-permute-start | bytes 442376 | tf_op jit(solution)/shard_map/ppermute | solution.py:159
  10.5 1.6 %collective-permute-start.12 = (bf16[576,128]{1,0:T(8,128)(2,1)S(1)}, bf16[576,128]{1,0:T(8,128)(2,1)S(1)}, u32[]{:S(2)}, u32[]{:S(2)}) collective-permute-start(bf16[576,128]{1,0:T(8,128)(2,1)S(1)} %get-tuple-element.15), channel_id=1, source_target_pairs={{0,4},{2,6},{4,0},{6,2},{8,12},{10,14},{12,8},{14,10},{1,5},{3,7},... | collective-permute-start | bytes 442376 | tf_op jit(solution)/shard_map/ppermute | solution.py:159
  12.1 2.6 %shard_map.70 = bf16[2304,128]{1,0:T(8,128)(2,1)S(1)} custom-call(bf16[512,256]{1,0:T(8,128)(2,1)S(1)} %bitcast.17, bf16[512,256]{1,0:T(8,128)(2,1)S(1)} %collective-permute-done.x_other, bf16[512,256]{1,0:T(8,128)(2,1)S(1)} %bitcast.14, bf16[512,256]{1,0:T(8,128)(2,1)S(1)} %collective-permute-done.1.c_other, bf16[2304,128]{1,0:T(8,128)(2,1)S(1)} %bitcast.10, ...), custom_call_target="tpu_custom_call" | custom-call | flops 1207959552 | bytes 2752512 | tf_op jit(solution)/shard_map/pallas_call | solution.py:146
  14.7 2.0 %collective-permute-start.4 = (bf16[576,128]{1,0:T(8,128)(2,1)S(1)}, bf16[576,128]{1,0:T(8,128)(2,1)S(1)}, u32[]{:S(2)}, u32[]{:S(2)}) collective-permute-start(bf16[576,128]{1,0:T(8,128)(2,1)S(1)} %get-tuple-element.16), channel_id=1, source_target_pairs={{0,2},{2,0},{4,6},{6,4},{8,10},{10,8},{12,14},{14,12},{1,3},{3,1},... | collective-permute-start | bytes 442376 | tf_op jit(solution)/shard_map/ppermute | solution.py:159
  16.7 1.6 %collective-permute-start.5 = (bf16[576,128]{1,0:T(8,128)(2,1)S(1)}, bf16[576,128]{1,0:T(8,128)(2,1)S(1)}, u32[]{:S(2)}, u32[]{:S(2)}) collective-permute-start(bf16[576,128]{1,0:T(8,128)(2,1)S(1)} %get-tuple-element.18), channel_id=1, source_target_pairs={{0,4},{2,6},{4,0},{6,2},{8,12},{10,14},{12,8},{14,10},{1,5},{3,7},... | collective-permute-start | bytes 442376 | tf_op jit(solution)/shard_map/ppermute | solution.py:159
  18.3 1.8 %shard_map.69 = bf16[512,256]{1,0:T(8,128)(2,1)} custom-call(bf16[512,256]{1,0:T(8,128)(2,1)S(1)} %bitcast.18, bf16[512,256]{1,0:T(8,128)(2,1)S(1)} %get-tuple-element.6.h_ref, bf16[2304,128]{1,0:T(8,128)(2,1)S(1)} %bitcast.11, bf16[2304,128]{1,0:T(8,128)(2,1)S(1)} %collective-permute-done.3.w_other), custom_call_target="tpu_custom_call" | custom-call | flops 603979776 | bytes 1703936 | tf_op jit(solution)/shard_map/pallas_call | solution.py:146
  20.1 0.1 add_convert_fusion
  20.2 3.0 %collective-permute-start.14 = (bf16[576,128]{1,0:T(8,128)(2,1)S(1)}, bf16[576,128]{1,0:T(8,128)(2,1)S(1)}, u32[]{:S(2)}, u32[]{:S(2)}) collective-permute-start(bf16[576,128]{1,0:T(8,128)(2,1)S(1)} %add_convert_fusion), channel_id=1, source_target_pairs={{0,8},{2,10},{4,12},{6,14},{8,0},{10,2},{12,4},{14,6},{1,9},{3,11}... | collective-permute-start | bytes 442376 | tf_op jit(solution)/shard_map/ppermute | solution.py:159
  23.3 3.4 %collective-permute-done.5 = bf16[576,128]{1,0:T(8,128)(2,1)S(1)} collective-permute-done((bf16[576,128]{1,0:T(8,128)(2,1)S(1)}, bf16[576,128]{1,0:T(8,128)(2,1)S(1)}, u32[]{:S(2)}, u32[]{:S(2)}) %collective-permute-start.5) | collective-permute-done | bytes 147488 | tf_op jit(solution)/shard_map/ppermute | solution.py:159
  26.6 0.9 %collective-permute-done.6 = bf16[576,128]{1,0:T(8,128)(2,1)S(1)} collective-permute-done((bf16[576,128]{1,0:T(8,128)(2,1)S(1)}, bf16[576,128]{1,0:T(8,128)(2,1)S(1)}, u32[]{:S(2)}, u32[]{:S(2)}) %collective-permute-start.6) | collective-permute-done | bytes 147488 | tf_op jit(solution)/shard_map/ppermute | solution.py:159
  27.5 0.1 add_convert_fusion.1
  27.6 2.3 %collective-permute-start.7 = (bf16[576,128]{1,0:T(8,128)(2,1)S(1)}, bf16[576,128]{1,0:T(8,128)(2,1)S(1)}, u32[]{:S(2)}, u32[]{:S(2)}) collective-permute-start(bf16[576,128]{1,0:T(8,128)(2,1)S(1)} %add_convert_fusion.1), channel_id=1, source_target_pairs={{0,8},{2,10},{4,12},{6,14},{8,0},{10,2},{12,4},{14,6},{1,9},{3,11}... | collective-permute-start | bytes 442376 | tf_op jit(solution)/shard_map/ppermute | solution.py:159
  29.9 0.1 broadcast.7.clone.1
  30.0 0.1 constant_dynamic-update-slice_fusion.3
  30.1 1.2 %collective-permute-start.15 = (bf16[576,128]{1,0:T(8,128)(2,1)S(1)}, bf16[576,128]{1,0:T(8,128)(2,1)S(1)}, u32[]{:S(2)}, u32[]{:S(2)}) collective-permute-start(bf16[576,128]{1,0:T(8,128)(2,1)S(1)} %get-tuple-element.10), channel_id=1, source_target_pairs={{0,2},{2,0},{4,6},{6,4},{8,10},{10,8},{12,14},{14,12},{1,3},{3,1},... | collective-permute-start | bytes 442376 | tf_op jit(solution)/shard_map/ppermute | solution.py:159
  31.3 2.7 %collective-permute-start.16 = (bf16[576,128]{1,0:T(8,128)(2,1)S(1)}, bf16[576,128]{1,0:T(8,128)(2,1)S(1)}, u32[]{:S(2)}, u32[]{:S(2)}) collective-permute-start(bf16[576,128]{1,0:T(8,128)(2,1)S(1)} %get-tuple-element.10), channel_id=1, source_target_pairs={{0,4},{2,6},{4,0},{6,2},{8,12},{10,14},{12,8},{14,10},{1,5},{3,7},... | collective-permute-start | bytes 442376 | tf_op jit(solution)/shard_map/ppermute | solution.py:159
  34.0 3.3 %collective-permute-done.7 = bf16[576,128]{1,0:T(8,128)(2,1)S(1)} collective-permute-done((bf16[576,128]{1,0:T(8,128)(2,1)S(1)}, bf16[576,128]{1,0:T(8,128)(2,1)S(1)}, u32[]{:S(2)}, u32[]{:S(2)}) %collective-permute-start.7) | collective-permute-done | bytes 147488 | tf_op jit(solution)/shard_map/ppermute | solution.py:159
  37.3 0.1 broadcast.7.clone
  37.4 0.1 constant_dynamic-update-slice_fusion.7
  37.4 2.3 %collective-permute-start.8 = (bf16[576,128]{1,0:T(8,128)(2,1)S(1)}, bf16[576,128]{1,0:T(8,128)(2,1)S(1)}, u32[]{:S(2)}, u32[]{:S(2)}) collective-permute-start(bf16[576,128]{1,0:T(8,128)(2,1)S(1)} %get-tuple-element.12), channel_id=1, source_target_pairs={{0,2},{2,0},{4,6},{6,4},{8,10},{10,8},{12,14},{14,12},{1,3},{3,1},... | collective-permute-start | bytes 442376 | tf_op jit(solution)/shard_map/ppermute | solution.py:159
  39.8 1.5 %collective-permute-start.10 = (bf16[576,128]{1,0:T(8,128)(2,1)S(1)}, bf16[576,128]{1,0:T(8,128)(2,1)S(1)}, u32[]{:S(2)}, u32[]{:S(2)}) collective-permute-start(bf16[576,128]{1,0:T(8,128)(2,1)S(1)} %get-tuple-element.12), channel_id=1, source_target_pairs={{0,6},{2,4},{4,2},{6,0},{8,14},{10,12},{12,10},{14,8},{1,7},{3,5},... | collective-permute-start | bytes 442376 | tf_op jit(solution)/shard_map/ppermute | solution.py:159
  41.4 1.9 %collective-permute-done.17 = bf16[576,128]{1,0:T(8,128)(2,1)S(1)} collective-permute-done((bf16[576,128]{1,0:T(8,128)(2,1)S(1)}, bf16[576,128]{1,0:T(8,128)(2,1)S(1)}, u32[]{:S(2)}, u32[]{:S(2)}) %collective-permute-start.17) | collective-permute-done | bytes 147488 | tf_op jit(solution)/shard_map/ppermute | solution.py:159
  43.4 2.9 %collective-permute-done.8 = bf16[576,128]{1,0:T(8,128)(2,1)S(1)} collective-permute-done((bf16[576,128]{1,0:T(8,128)(2,1)S(1)}, bf16[576,128]{1,0:T(8,128)(2,1)S(1)}, u32[]{:S(2)}, u32[]{:S(2)}) %collective-permute-start.8) | collective-permute-done | bytes 147488 | tf_op jit(solution)/shard_map/ppermute | solution.py:159
  46.2 0.3 collective-permute-done.9
  46.6 2.3 %collective-permute-done.10 = bf16[576,128]{1,0:T(8,128)(2,1)S(1)} collective-permute-done((bf16[576,128]{1,0:T(8,128)(2,1)S(1)}, bf16[576,128]{1,0:T(8,128)(2,1)S(1)}, u32[]{:S(2)}, u32[]{:S(2)}) %collective-permute-start.10) | collective-permute-done | bytes 147488 | tf_op jit(solution)/shard_map/ppermute | solution.py:159
  48.9 0.8 %copy-done.4 = bf16[2304,128]{1,0:T(8,128)(2,1)} copy-done((bf16[2304,128]{1,0:T(8,128)(2,1)}, bf16[2304,128]{1,0:T(8,128)(2,1)S(1)}, u32[]{:S(2)}) %copy-start.4) | copy-done | bytes 589848
  (34 shorter events, 0.4 us)
Async XLA Ops:
  0.6 4.0 %collective-permute-start.2 = (bf16[2304,128]{1,0:T(8,128)(2,1)}, bf16[2304,128]{1,0:T(8,128)(2,1)S(1)}, u32[]{:S(2)}, u32[]{:S(2)}) collective-permute-start(bf16[2304,128]{1,0:T(8,128)(2,1)} %bitcast.7), channel_id=1, source_target_pairs={{0,1},{1,0},{2,3},{3,2},{4,5},{5,4},{6,7},{7,6},{8,9},{9,8},{10,11... | collective-permute-start | bytes 1769480 | tf_op jit(solution)/shard_map/ppermute | solution.py:224
  1.1 11.0 %collective-permute-start.3 = (bf16[2304,128]{1,0:T(8,128)(2,1)}, bf16[2304,128]{1,0:T(8,128)(2,1)S(1)}, u32[]{:S(2)}, u32[]{:S(2)}) collective-permute-start(bf16[2304,128]{1,0:T(8,128)(2,1)} %bitcast.9), channel_id=1, source_target_pairs={{0,1},{1,0},{2,3},{3,2},{4,5},{5,4},{6,7},{7,6},{8,9},{9,8},{10,11... | collective-permute-start | bytes 1769480 | tf_op jit(solution)/shard_map/ppermute | solution.py:224
  1.2 3.0 %collective-permute-start = (bf16[512,256]{1,0:T(8,128)(2,1)}, bf16[512,256]{1,0:T(8,128)(2,1)S(1)}, u32[]{:S(2)}, u32[]{:S(2)}) collective-permute-start(bf16[512,256]{1,0:T(8,128)(2,1)} %bitcast.15), channel_id=1, source_target_pairs={{0,1},{1,0},{2,3},{3,2},{4,5},{5,4},{6,7},{7,6},{8,9},{9,8},{10,11... | collective-permute-start | bytes 786440 | tf_op jit(solution)/shard_map/ppermute | solution.py:224
  1.7 2.9 %collective-permute-start.1 = (bf16[512,256]{1,0:T(8,128)(2,1)}, bf16[512,256]{1,0:T(8,128)(2,1)S(1)}, u32[]{:S(2)}, u32[]{:S(2)}) collective-permute-start(bf16[512,256]{1,0:T(8,128)(2,1)} %bitcast.12), channel_id=1, source_target_pairs={{0,1},{1,0},{2,3},{3,2},{4,5},{5,4},{6,7},{7,6},{8,9},{9,8},{10,11... | collective-permute-start | bytes 786440 | tf_op jit(solution)/shard_map/ppermute | solution.py:224
  1.7 2.9 %copy-start = (bf16[9,256,128]{2,1,0:T(8,128)(2,1)S(1)}, bf16[9,256,128]{2,1,0:T(8,128)(2,1)}, u32[]{:S(2)}) copy-start(bf16[9,256,128]{2,1,0:T(8,128)(2,1)} %param.6) | copy-start | bytes 1769476
  1.7 2.9 %copy-start.2 = (bf16[1,16,32,256]{3,2,1,0:T(8,128)(2,1)S(1)}, bf16[1,16,32,256]{3,2,1,0:T(8,128)(2,1)}, u32[]{:S(2)}) copy-start(bf16[1,16,32,256]{3,2,1,0:T(8,128)(2,1)} %param.5) | copy-start | bytes 786436
  1.7 2.9 %copy-start.3 = (bf16[1,16,32,256]{3,2,1,0:T(8,128)(2,1)S(1)}, bf16[1,16,32,256]{3,2,1,0:T(8,128)(2,1)}, u32[]{:S(2)}) copy-start(bf16[1,16,32,256]{3,2,1,0:T(8,128)(2,1)} %param.4) | copy-start | bytes 786436
  7.5 4.6 %copy-start.1 = (bf16[9,256,128]{2,1,0:T(8,128)(2,1)S(1)}, bf16[9,256,128]{2,1,0:T(8,128)(2,1)}, u32[]{:S(2)}) copy-start(bf16[9,256,128]{2,1,0:T(8,128)(2,1)} %param.7) | copy-start | bytes 1769476
  7.6 12.5 %collective-permute-start.11 = (bf16[576,128]{1,0:T(8,128)(2,1)S(1)}, bf16[576,128]{1,0:T(8,128)(2,1)S(1)}, u32[]{:S(2)}, u32[]{:S(2)}) collective-permute-start(bf16[576,128]{1,0:T(8,128)(2,1)S(1)} %get-tuple-element.13), channel_id=1, source_target_pairs={{0,2},{2,0},{4,6},{6,4},{8,10},{10,8},{12,14},{14,12},{1,3},{3,1},... | collective-permute-start | bytes 442376 | tf_op jit(solution)/shard_map/ppermute | solution.py:159
  10.5 9.6 %collective-permute-start.12 = (bf16[576,128]{1,0:T(8,128)(2,1)S(1)}, bf16[576,128]{1,0:T(8,128)(2,1)S(1)}, u32[]{:S(2)}, u32[]{:S(2)}) collective-permute-start(bf16[576,128]{1,0:T(8,128)(2,1)S(1)} %get-tuple-element.15), channel_id=1, source_target_pairs={{0,4},{2,6},{4,0},{6,2},{8,12},{10,14},{12,8},{14,10},{1,5},{3,7},... | collective-permute-start | bytes 442376 | tf_op jit(solution)/shard_map/ppermute | solution.py:159
  12.1 8.0 %collective-permute-start.13 = (bf16[576,128]{1,0:T(8,128)(2,1)S(1)}, bf16[576,128]{1,0:T(8,128)(2,1)S(1)}, u32[]{:S(2)}, u32[]{:S(2)}) collective-permute-start(bf16[576,128]{1,0:T(8,128)(2,1)S(1)} %get-tuple-element.14), channel_id=1, source_target_pairs={{0,6},{2,4},{4,2},{6,0},{8,14},{10,12},{12,10},{14,8},{1,7},{3,5},... | collective-permute-start | bytes 442376 | tf_op jit(solution)/shard_map/ppermute | solution.py:159
  14.7 8.5 %collective-permute-start.4 = (bf16[576,128]{1,0:T(8,128)(2,1)S(1)}, bf16[576,128]{1,0:T(8,128)(2,1)S(1)}, u32[]{:S(2)}, u32[]{:S(2)}) collective-permute-start(bf16[576,128]{1,0:T(8,128)(2,1)S(1)} %get-tuple-element.16), channel_id=1, source_target_pairs={{0,2},{2,0},{4,6},{6,4},{8,10},{10,8},{12,14},{14,12},{1,3},{3,1},... | collective-permute-start | bytes 442376 | tf_op jit(solution)/shard_map/ppermute | solution.py:159
  16.7 9.9 %collective-permute-start.5 = (bf16[576,128]{1,0:T(8,128)(2,1)S(1)}, bf16[576,128]{1,0:T(8,128)(2,1)S(1)}, u32[]{:S(2)}, u32[]{:S(2)}) collective-permute-start(bf16[576,128]{1,0:T(8,128)(2,1)S(1)} %get-tuple-element.18), channel_id=1, source_target_pairs={{0,4},{2,6},{4,0},{6,2},{8,12},{10,14},{12,8},{14,10},{1,5},{3,7},... | collective-permute-start | bytes 442376 | tf_op jit(solution)/shard_map/ppermute | solution.py:159
  20.1 7.4 %collective-permute-start.6 = (bf16[576,128]{1,0:T(8,128)(2,1)S(1)}, bf16[576,128]{1,0:T(8,128)(2,1)S(1)}, u32[]{:S(2)}, u32[]{:S(2)}) collective-permute-start(bf16[576,128]{1,0:T(8,128)(2,1)S(1)} %get-tuple-element.17), channel_id=1, source_target_pairs={{0,6},{2,4},{4,2},{6,0},{8,14},{10,12},{12,10},{14,8},{1,7},{3,5},... | collective-permute-start | bytes 442376 | tf_op jit(solution)/shard_map/ppermute | solution.py:159
  20.2 9.7 %collective-permute-start.14 = (bf16[576,128]{1,0:T(8,128)(2,1)S(1)}, bf16[576,128]{1,0:T(8,128)(2,1)S(1)}, u32[]{:S(2)}, u32[]{:S(2)}) collective-permute-start(bf16[576,128]{1,0:T(8,128)(2,1)S(1)} %add_convert_fusion), channel_id=1, source_target_pairs={{0,8},{2,10},{4,12},{6,14},{8,0},{10,2},{12,4},{14,6},{1,9},{3,11}... | collective-permute-start | bytes 442376 | tf_op jit(solution)/shard_map/ppermute | solution.py:159
  27.6 9.7 %collective-permute-start.7 = (bf16[576,128]{1,0:T(8,128)(2,1)S(1)}, bf16[576,128]{1,0:T(8,128)(2,1)S(1)}, u32[]{:S(2)}, u32[]{:S(2)}) collective-permute-start(bf16[576,128]{1,0:T(8,128)(2,1)S(1)} %add_convert_fusion.1), channel_id=1, source_target_pairs={{0,8},{2,10},{4,12},{6,14},{8,0},{10,2},{12,4},{14,6},{1,9},{3,11}... | collective-permute-start | bytes 442376 | tf_op jit(solution)/shard_map/ppermute | solution.py:159
  30.1 9.7 %collective-permute-start.15 = (bf16[576,128]{1,0:T(8,128)(2,1)S(1)}, bf16[576,128]{1,0:T(8,128)(2,1)S(1)}, u32[]{:S(2)}, u32[]{:S(2)}) collective-permute-start(bf16[576,128]{1,0:T(8,128)(2,1)S(1)} %get-tuple-element.10), channel_id=1, source_target_pairs={{0,2},{2,0},{4,6},{6,4},{8,10},{10,8},{12,14},{14,12},{1,3},{3,1},... | collective-permute-start | bytes 442376 | tf_op jit(solution)/shard_map/ppermute | solution.py:159
  31.3 10.0 %collective-permute-start.16 = (bf16[576,128]{1,0:T(8,128)(2,1)S(1)}, bf16[576,128]{1,0:T(8,128)(2,1)S(1)}, u32[]{:S(2)}, u32[]{:S(2)}) collective-permute-start(bf16[576,128]{1,0:T(8,128)(2,1)S(1)} %get-tuple-element.10), channel_id=1, source_target_pairs={{0,4},{2,6},{4,0},{6,2},{8,12},{10,14},{12,8},{14,10},{1,5},{3,7},... | collective-permute-start | bytes 442376 | tf_op jit(solution)/shard_map/ppermute | solution.py:159
  34.0 9.3 %collective-permute-start.17 = (bf16[576,128]{1,0:T(8,128)(2,1)S(1)}, bf16[576,128]{1,0:T(8,128)(2,1)S(1)}, u32[]{:S(2)}, u32[]{:S(2)}) collective-permute-start(bf16[576,128]{1,0:T(8,128)(2,1)S(1)} %get-tuple-element.10), channel_id=1, source_target_pairs={{0,6},{2,4},{4,2},{6,0},{8,14},{10,12},{12,10},{14,8},{1,7},{3,5},... | collective-permute-start | bytes 442376 | tf_op jit(solution)/shard_map/ppermute | solution.py:159
  37.4 8.8 %collective-permute-start.8 = (bf16[576,128]{1,0:T(8,128)(2,1)S(1)}, bf16[576,128]{1,0:T(8,128)(2,1)S(1)}, u32[]{:S(2)}, u32[]{:S(2)}) collective-permute-start(bf16[576,128]{1,0:T(8,128)(2,1)S(1)} %get-tuple-element.12), channel_id=1, source_target_pairs={{0,2},{2,0},{4,6},{6,4},{8,10},{10,8},{12,14},{14,12},{1,3},{3,1},... | collective-permute-start | bytes 442376 | tf_op jit(solution)/shard_map/ppermute | solution.py:159
  39.8 6.8 %collective-permute-start.9 = (bf16[576,128]{1,0:T(8,128)(2,1)S(1)}, bf16[576,128]{1,0:T(8,128)(2,1)S(1)}, u32[]{:S(2)}, u32[]{:S(2)}) collective-permute-start(bf16[576,128]{1,0:T(8,128)(2,1)S(1)} %get-tuple-element.12), channel_id=1, source_target_pairs={{0,4},{2,6},{4,0},{6,2},{8,12},{10,14},{12,8},{14,10},{1,5},{3,7},... | collective-permute-start | bytes 442376 | tf_op jit(solution)/shard_map/ppermute | solution.py:159
  39.8 9.1 %collective-permute-start.10 = (bf16[576,128]{1,0:T(8,128)(2,1)S(1)}, bf16[576,128]{1,0:T(8,128)(2,1)S(1)}, u32[]{:S(2)}, u32[]{:S(2)}) collective-permute-start(bf16[576,128]{1,0:T(8,128)(2,1)S(1)} %get-tuple-element.12), channel_id=1, source_target_pairs={{0,6},{2,4},{4,2},{6,0},{8,14},{10,12},{12,10},{14,8},{1,7},{3,5},... | collective-permute-start | bytes 442376 | tf_op jit(solution)/shard_map/ppermute | solution.py:159
  43.3 5.6 %copy-start.5 = (bf16[2304,128]{1,0:T(8,128)(2,1)}, bf16[2304,128]{1,0:T(8,128)(2,1)S(1)}, u32[]{:S(2)}) copy-start(bf16[2304,128]{1,0:T(8,128)(2,1)S(1)} %constant_dynamic-update-slice_fusion) | copy-start | bytes 1769476
  48.9 0.8 %copy-start.4 = (bf16[2304,128]{1,0:T(8,128)(2,1)}, bf16[2304,128]{1,0:T(8,128)(2,1)S(1)}, u32[]{:S(2)}) copy-start(bf16[2304,128]{1,0:T(8,128)(2,1)S(1)} %constant_dynamic-update-slice_fusion.4) | copy-start | bytes 1769476

commit v4 on v3

--- a/solution.py
+++ b/solution.py
@@ -47,7 +47,7 @@
 def first_kernel(
     cols, x_own, x_other, c_own, c_other, w_own, w_other, ready_ref,
     grad_ref, hidden_ref, slope_ref,
-    weight, taps, narrow, turned, pre_ref,
+    weight, taps, narrow, turned, pre_ref, sg_ref,
 ):
     cells, chans = x_own.shape
     half = w_own.shape[1]
@@ -63,12 +63,14 @@
                 preferred_element_type=F32,
             )
         pre_ref[...] = pre
-        hidden = pre * jax.nn.sigmoid(pre)
+        sg_all = jax.nn.sigmoid(pre)
+        sg_ref[...] = sg_all
+        hidden = pre * sg_all
         if sample == 0:
             hidden_ref[...] = hidden.astype(BF16)
-        turned[:, sample * cells : (sample + 1) * cells] = hidden.T.astype(BF16)
+        turned[:, sample * cells : (sample + 1) * cells] = hidden.astype(BF16).T
         mine = pre_ref[:, pl.ds(start, half)]
-        sg = jax.nn.sigmoid(mine)
+        sg = sg_ref[:, pl.ds(start, half)]
         slope_ref[sample * cells : (sample + 1) * cells, :] = sg * (1.0 + mine * (1.0 - sg))
         fill_taps(narrow.at[sample], c_ref[:, pl.ds(start, half)].astype(F32), cols, (1, 0, -1))
     weight_grad(cols, turned, narrow, grad_ref)
@@ -238,7 +240,7 @@
             jax.ShapeDtypeStruct((cells, chans), BF16),
             jax.ShapeDtypeStruct((2 * cells, half), F32),
         ),
-        [weight, taps, narrow, turned, pltpu.VMEM((cells, chans), F32)],
+        [weight, taps, narrow, turned, pltpu.VMEM((cells, chans), F32), pltpu.VMEM((cells, chans), F32)],
         3 * unit,
         x_own, x_other, c_own, c_other, w1_own, w1_other, ready,
     )

time: 49.9 us -> 49.9 us (level)
  no operation moved by 1% of the time
where the time goes in v4:
time: 49.9 us; the launch traced here: 49.8 us
  starting transfers between devices  22.3 us (45%)
  waiting for transfers between devices  17.8 us (36%)
  Pallas kernels  7.34 us (15%)
  local copies, waits for them, and re-layouts  1.19 us (2%)
  between operations  0.78 us (2%)
    ppermute x14, starting transfers between devices, swapped(): return lax.ppermute(value, 'dp', pairs)  21.2 us
    ppermute x14, waiting for transfers between devices, swapped(): return lax.ppermute(value, 'dp', pairs)  15 us
    pallas_call x4, Pallas kernels, call(): pl.pallas_call(functools.partial(kernel, cols), out_shape=outs, in_specs=...  7.34 us
    ppermute x4, waiting for transfers between devices, body(): lax.ppermute(v, 'shard', swap)  2.84 us
    ppermute x4, starting transfers between devices, body(): lax.ppermute(v, 'shard', swap)  1.11 us
  transfers between devices with their start and end apart: 18, of which 9 were waited for; matrix products, arithmetic and copies ran while one was open for 1% of the time, Pallas kernels for 15%

profile of v4, /device:TPU:0, one launch (start us, length us, event | category | flops | bytes accessed | tf_op | source)
XLA Modules:
  0.0 49.8 jit_solution(12630290573769250317)
XLA Ops:
  0.6 0.5 %collective-permute-start.2 = (bf16[2304,128]{1,0:T(8,128)(2,1)}, bf16[2304,128]{1,0:T(8,128)(2,1)S(1)}, u32[]{:S(2)}, u32[]{:S(2)}) collective-permute-start(bf16[2304,128]{1,0:T(8,128)(2,1)} %bitcast.7), channel_id=1, source_target_pairs={{0,1},{1,0},{2,3},{3,2},{4,5},{5,4},{6,7},{7,6},{8,9},{9,8},{10,11... | collective-permute-start | bytes 1769480 | tf_op jit(solution)/shard_map/ppermute | solution.py:226
  1.2 0.4 collective-permute-start
  1.7 0.1 collective-permute-start.1
  1.7 2.5 %collective-permute-done.x_other = bf16[512,256]{1,0:T(8,128)(2,1)S(1)} collective-permute-done((bf16[512,256]{1,0:T(8,128)(2,1)}, bf16[512,256]{1,0:T(8,128)(2,1)S(1)}, u32[]{:S(2)}, u32[]{:S(2)}) %collective-permute-start) | collective-permute-done | bytes 262176 | tf_op jit(solution)/shard_map/ppermute | solution.py:226
  4.2 0.4 collective-permute-done.1.c_other
  4.6 3.0 %shard_map.68 = (bf16[2304,128]{1,0:T(8,128)(2,1)S(1)}, bf16[512,256]{1,0:T(8,128)(2,1)S(1)}, f32[1024,128]{1,0:T(8,128)S(1)}) custom-call(bf16[512,256]{1,0:T(8,128)(2,1)S(1)} %bitcast.16, bf16[512,256]{1,0:T(8,128)(2,1)S(1)} %collective-permute-done.x_other, bf16[512,256]{1,0:T(8,128)(2,1)S(1)} %bitcast.13, ...), custom_call_target="tpu_custom_call" | custom-call | flops 1811939328 | bytes 2232320 | tf_op jit(solution)/shard_map/pallas_call | solution.py:148
  7.6 2.9 %collective-permute-start.11 = (bf16[576,128]{1,0:T(8,128)(2,1)S(1)}, bf16[576,128]{1,0:T(8,128)(2,1)S(1)}, u32[]{:S(2)}, u32[]{:S(2)}) collective-permute-start(bf16[576,128]{1,0:T(8,128)(2,1)S(1)} %get-tuple-element.13), channel_id=1, source_target_pairs={{0,2},{2,0},{4,6},{6,4},{8,10},{10,8},{12,14},{14,12},{1,3},{3,1},... | collective-permute-start | bytes 442376 | tf_op jit(solution)/shard_map/ppermute | solution.py:161
  10.6 1.6 %collective-permute-start.12 = (bf16[576,128]{1,0:T(8,128)(2,1)S(1)}, bf16[576,128]{1,0:T(8,128)(2,1)S(1)}, u32[]{:S(2)}, u32[]{:S(2)}) collective-permute-start(bf16[576,128]{1,0:T(8,128)(2,1)S(1)} %get-tuple-element.15), channel_id=1, source_target_pairs={{0,4},{2,6},{4,0},{6,2},{8,12},{10,14},{12,8},{14,10},{1,5},{3,7},... | collective-permute-start | bytes 442376 | tf_op jit(solution)/shard_map/ppermute | solution.py:161
  12.2 2.6 %shard_map.70 = bf16[2304,128]{1,0:T(8,128)(2,1)S(1)} custom-call(bf16[512,256]{1,0:T(8,128)(2,1)S(1)} %bitcast.17, bf16[512,256]{1,0:T(8,128)(2,1)S(1)} %collective-permute-done.x_other, bf16[512,256]{1,0:T(8,128)(2,1)S(1)} %bitcast.14, bf16[512,256]{1,0:T(8,128)(2,1)S(1)} %collective-permute-done.1.c_other, bf16[2304,128]{1,0:T(8,128)(2,1)S(1)} %bitcast.10, ...), custom_call_target="tpu_custom_call" | custom-call | flops 1207959552 | bytes 2752512 | tf_op jit(solution)/shard_map/pallas_call | solution.py:148
  14.8 2.0 %collective-permute-start.4 = (bf16[576,128]{1,0:T(8,128)(2,1)S(1)}, bf16[576,128]{1,0:T(8,128)(2,1)S(1)}, u32[]{:S(2)}, u32[]{:S(2)}) collective-permute-start(bf16[576,128]{1,0:T(8,128)(2,1)S(1)} %get-tuple-element.16), channel_id=1, source_target_pairs={{0,2},{2,0},{4,6},{6,4},{8,10},{10,8},{12,14},{14,12},{1,3},{3,1},... | collective-permute-start | bytes 442376 | tf_op jit(solution)/shard_map/ppermute | solution.py:161
  16.7 1.6 %collective-permute-start.5 = (bf16[576,128]{1,0:T(8,128)(2,1)S(1)}, bf16[576,128]{1,0:T(8,128)(2,1)S(1)}, u32[]{:S(2)}, u32[]{:S(2)}) collective-permute-start(bf16[576,128]{1,0:T(8,128)(2,1)S(1)} %get-tuple-element.18), channel_id=1, source_target_pairs={{0,4},{2,6},{4,0},{6,2},{8,12},{10,14},{12,8},{14,10},{1,5},{3,7},... | collective-permute-start | bytes 442376 | tf_op jit(solution)/shard_map/ppermute | solution.py:161
  18.3 1.8 %shard_map.69 = bf16[512,256]{1,0:T(8,128)(2,1)} custom-call(bf16[512,256]{1,0:T(8,128)(2,1)S(1)} %bitcast.18, bf16[512,256]{1,0:T(8,128)(2,1)S(1)} %get-tuple-element.6.h_ref, bf16[2304,128]{1,0:T(8,128)(2,1)S(1)} %bitcast.11, bf16[2304,128]{1,0:T(8,128)(2,1)S(1)} %collective-permute-done.3.w_other), custom_call_target="tpu_custom_call" | custom-call | flops 603979776 | bytes 1703936 | tf_op jit(solution)/shard_map/pallas_call | solution.py:148
  20.1 0.1 add_convert_fusion
  20.2 3.0 %collective-permute-start.14 = (bf16[576,128]{1,0:T(8,128)(2,1)S(1)}, bf16[576,128]{1,0:T(8,128)(2,1)S(1)}, u32[]{:S(2)}, u32[]{:S(2)}) collective-permute-start(bf16[576,128]{1,0:T(8,128)(2,1)S(1)} %add_convert_fusion), channel_id=1, source_target_pairs={{0,8},{2,10},{4,12},{6,14},{8,0},{10,2},{12,4},{14,6},{1,9},{3,11}... | collective-permute-start | bytes 442376 | tf_op jit(solution)/shard_map/ppermute | solution.py:161
  23.3 3.4 %collective-permute-done.5 = bf16[576,128]{1,0:T(8,128)(2,1)S(1)} collective-permute-done((bf16[576,128]{1,0:T(8,128)(2,1)S(1)}, bf16[576,128]{1,0:T(8,128)(2,1)S(1)}, u32[]{:S(2)}, u32[]{:S(2)}) %collective-permute-start.5) | collective-permute-done | bytes 147488 | tf_op jit(solution)/shard_map/ppermute | solution.py:161
  26.7 0.9 %collective-permute-done.6 = bf16[576,128]{1,0:T(8,128)(2,1)S(1)} collective-permute-done((bf16[576,128]{1,0:T(8,128)(2,1)S(1)}, bf16[576,128]{1,0:T(8,128)(2,1)S(1)}, u32[]{:S(2)}, u32[]{:S(2)}) %collective-permute-start.6) | collective-permute-done | bytes 147488 | tf_op jit(solution)/shard_map/ppermute | solution.py:161
  27.6 0.1 add_convert_fusion.1
  27.7 2.3 %collective-permute-start.7 = (bf16[576,128]{1,0:T(8,128)(2,1)S(1)}, bf16[576,128]{1,0:T(8,128)(2,1)S(1)}, u32[]{:S(2)}, u32[]{:S(2)}) collective-permute-start(bf16[576,128]{1,0:T(8,128)(2,1)S(1)} %add_convert_fusion.1), channel_id=1, source_target_pairs={{0,8},{2,10},{4,12},{6,14},{8,0},{10,2},{12,4},{14,6},{1,9},{3,11}... | collective-permute-start | bytes 442376 | tf_op jit(solution)/shard_map/ppermute | solution.py:161
  30.0 0.1 broadcast.7.clone.1
  30.0 0.1 constant_dynamic-update-slice_fusion.3
  30.1 1.2 %collective-permute-start.15 = (bf16[576,128]{1,0:T(8,128)(2,1)S(1)}, bf16[576,128]{1,0:T(8,128)(2,1)S(1)}, u32[]{:S(2)}, u32[]{:S(2)}) collective-permute-start(bf16[576,128]{1,0:T(8,128)(2,1)S(1)} %get-tuple-element.10), channel_id=1, source_target_pairs={{0,2},{2,0},{4,6},{6,4},{8,10},{10,8},{12,14},{14,12},{1,3},{3,1},... | collective-permute-start | bytes 442376 | tf_op jit(solution)/shard_map/ppermute | solution.py:161
  31.3 2.7 %collective-permute-start.16 = (bf16[576,128]{1,0:T(8,128)(2,1)S(1)}, bf16[576,128]{1,0:T(8,128)(2,1)S(1)}, u32[]{:S(2)}, u32[]{:S(2)}) collective-permute-start(bf16[576,128]{1,0:T(8,128)(2,1)S(1)} %get-tuple-element.10), channel_id=1, source_target_pairs={{0,4},{2,6},{4,0},{6,2},{8,12},{10,14},{12,8},{14,10},{1,5},{3,7},... | collective-permute-start | bytes 442376 | tf_op jit(solution)/shard_map/ppermute | solution.py:161
  34.0 3.3 %collective-permute-done.7 = bf16[576,128]{1,0:T(8,128)(2,1)S(1)} collective-permute-done((bf16[576,128]{1,0:T(8,128)(2,1)S(1)}, bf16[576,128]{1,0:T(8,128)(2,1)S(1)}, u32[]{:S(2)}, u32[]{:S(2)}) %collective-permute-start.7) | collective-permute-done | bytes 147488 | tf_op jit(solution)/shard_map/ppermute | solution.py:161
  37.3 0.1 broadcast.7.clone
  37.4 0.1 constant_dynamic-update-slice_fusion.7
  37.5 2.3 %collective-permute-start.8 = (bf16[576,128]{1,0:T(8,128)(2,1)S(1)}, bf16[576,128]{1,0:T(8,128)(2,1)S(1)}, u32[]{:S(2)}, u32[]{:S(2)}) collective-permute-start(bf16[576,128]{1,0:T(8,128)(2,1)S(1)} %get-tuple-element.12), channel_id=1, source_target_pairs={{0,2},{2,0},{4,6},{6,4},{8,10},{10,8},{12,14},{14,12},{1,3},{3,1},... | collective-permute-start | bytes 442376 | tf_op jit(solution)/shard_map/ppermute | solution.py:161
  39.8 1.5 %collective-permute-start.10 = (bf16[576,128]{1,0:T(8,128)(2,1)S(1)}, bf16[576,128]{1,0:T(8,128)(2,1)S(1)}, u32[]{:S(2)}, u32[]{:S(2)}) collective-permute-start(bf16[576,128]{1,0:T(8,128)(2,1)S(1)} %get-tuple-element.12), channel_id=1, source_target_pairs={{0,6},{2,4},{4,2},{6,0},{8,14},{10,12},{12,10},{14,8},{1,7},{3,5},... | collective-permute-start | bytes 442376 | tf_op jit(solution)/shard_map/ppermute | solution.py:161
  41.4 2.0 %collective-permute-done.17 = bf16[576,128]{1,0:T(8,128)(2,1)S(1)} collective-permute-done((bf16[576,128]{1,0:T(8,128)(2,1)S(1)}, bf16[576,128]{1,0:T(8,128)(2,1)S(1)}, u32[]{:S(2)}, u32[]{:S(2)}) %collective-permute-start.17) | collective-permute-done | bytes 147488 | tf_op jit(solution)/shard_map/ppermute | solution.py:161
  43.4 2.8 %collective-permute-done.8 = bf16[576,128]{1,0:T(8,128)(2,1)S(1)} collective-permute-done((bf16[576,128]{1,0:T(8,128)(2,1)S(1)}, bf16[576,128]{1,0:T(8,128)(2,1)S(1)}, u32[]{:S(2)}, u32[]{:S(2)}) %collective-permute-start.8) | collective-permute-done | bytes 147488 | tf_op jit(solution)/shard_map/ppermute | solution.py:161
  46.3 0.3 collective-permute-done.9
  46.6 2.3 %collective-permute-done.10 = bf16[576,128]{1,0:T(8,128)(2,1)S(1)} collective-permute-done((bf16[576,128]{1,0:T(8,128)(2,1)S(1)}, bf16[576,128]{1,0:T(8,128)(2,1)S(1)}, u32[]{:S(2)}, u32[]{:S(2)}) %collective-permute-start.10) | collective-permute-done | bytes 147488 | tf_op jit(solution)/shard_map/ppermute | solution.py:161
  49.0 0.8 %copy-done.4 = bf16[2304,128]{1,0:T(8,128)(2,1)} copy-done((bf16[2304,128]{1,0:T(8,128)(2,1)}, bf16[2304,128]{1,0:T(8,128)(2,1)S(1)}, u32[]{:S(2)}) %copy-start.4) | copy-done | bytes 589848
  (34 shorter events, 0.4 us)
Async XLA Ops:
  0.6 4.0 %collective-permute-start.2 = (bf16[2304,128]{1,0:T(8,128)(2,1)}, bf16[2304,128]{1,0:T(8,128)(2,1)S(1)}, u32[]{:S(2)}, u32[]{:S(2)}) collective-permute-start(bf16[2304,128]{1,0:T(8,128)(2,1)} %bitcast.7), channel_id=1, source_target_pairs={{0,1},{1,0},{2,3},{3,2},{4,5},{5,4},{6,7},{7,6},{8,9},{9,8},{10,11... | collective-permute-start | bytes 1769480 | tf_op jit(solution)/shard_map/ppermute | solution.py:226
  1.1 11.0 %collective-permute-start.3 = (bf16[2304,128]{1,0:T(8,128)(2,1)}, bf16[2304,128]{1,0:T(8,128)(2,1)S(1)}, u32[]{:S(2)}, u32[]{:S(2)}) collective-permute-start(bf16[2304,128]{1,0:T(8,128)(2,1)} %bitcast.9), channel_id=1, source_target_pairs={{0,1},{1,0},{2,3},{3,2},{4,5},{5,4},{6,7},{7,6},{8,9},{9,8},{10,11... | collective-permute-start | bytes 1769480 | tf_op jit(solution)/shard_map/ppermute | solution.py:226
  1.2 3.0 %collective-permute-start = (bf16[512,256]{1,0:T(8,128)(2,1)}, bf16[512,256]{1,0:T(8,128)(2,1)S(1)}, u32[]{:S(2)}, u32[]{:S(2)}) collective-permute-start(bf16[512,256]{1,0:T(8,128)(2,1)} %bitcast.15), channel_id=1, source_target_pairs={{0,1},{1,0},{2,3},{3,2},{4,5},{5,4},{6,7},{7,6},{8,9},{9,8},{10,11... | collective-permute-start | bytes 786440 | tf_op jit(solution)/shard_map/ppermute | solution.py:226
  1.7 2.9 %collective-permute-start.1 = (bf16[512,256]{1,0:T(8,128)(2,1)}, bf16[512,256]{1,0:T(8,128)(2,1)S(1)}, u32[]{:S(2)}, u32[]{:S(2)}) collective-permute-start(bf16[512,256]{1,0:T(8,128)(2,1)} %bitcast.12), channel_id=1, source_target_pairs={{0,1},{1,0},{2,3},{3,2},{4,5},{5,4},{6,7},{7,6},{8,9},{9,8},{10,11... | collective-permute-start | bytes 786440 | tf_op jit(solution)/shard_map/ppermute | solution.py:226
  1.7 2.9 %copy-start = (bf16[9,256,128]{2,1,0:T(8,128)(2,1)S(1)}, bf16[9,256,128]{2,1,0:T(8,128)(2,1)}, u32[]{:S(2)}) copy-start(bf16[9,256,128]{2,1,0:T(8,128)(2,1)} %param.6) | copy-start | bytes 1769476
  1.7 2.9 %copy-start.2 = (bf16[1,16,32,256]{3,2,1,0:T(8,128)(2,1)S(1)}, bf16[1,16,32,256]{3,2,1,0:T(8,128)(2,1)}, u32[]{:S(2)}) copy-start(bf16[1,16,32,256]{3,2,1,0:T(8,128)(2,1)} %param.5) | copy-start | bytes 786436
  1.7 2.9 %copy-start.3 = (bf16[1,16,32,256]{3,2,1,0:T(8,128)(2,1)S(1)}, bf16[1,16,32,256]{3,2,1,0:T(8,128)(2,1)}, u32[]{:S(2)}) copy-start(bf16[1,16,32,256]{3,2,1,0:T(8,128)(2,1)} %param.4) | copy-start | bytes 786436
  7.6 4.6 %copy-start.1 = (bf16[9,256,128]{2,1,0:T(8,128)(2,1)S(1)}, bf16[9,256,128]{2,1,0:T(8,128)(2,1)}, u32[]{:S(2)}) copy-start(bf16[9,256,128]{2,1,0:T(8,128)(2,1)} %param.7) | copy-start | bytes 1769476
  7.6 12.5 %collective-permute-start.11 = (bf16[576,128]{1,0:T(8,128)(2,1)S(1)}, bf16[576,128]{1,0:T(8,128)(2,1)S(1)}, u32[]{:S(2)}, u32[]{:S(2)}) collective-permute-start(bf16[576,128]{1,0:T(8,128)(2,1)S(1)} %get-tuple-element.13), channel_id=1, source_target_pairs={{0,2},{2,0},{4,6},{6,4},{8,10},{10,8},{12,14},{14,12},{1,3},{3,1},... | collective-permute-start | bytes 442376 | tf_op jit(solution)/shard_map/ppermute | solution.py:161
  10.6 9.6 %collective-permute-start.12 = (bf16[576,128]{1,0:T(8,128)(2,1)S(1)}, bf16[576,128]{1,0:T(8,128)(2,1)S(1)}, u32[]{:S(2)}, u32[]{:S(2)}) collective-permute-start(bf16[576,128]{1,0:T(8,128)(2,1)S(1)} %get-tuple-element.15), channel_id=1, source_target_pairs={{0,4},{2,6},{4,0},{6,2},{8,12},{10,14},{12,8},{14,10},{1,5},{3,7},... | collective-permute-start | bytes 442376 | tf_op jit(solution)/shard_map/ppermute | solution.py:161
  12.1 8.0 %collective-permute-start.13 = (bf16[576,128]{1,0:T(8,128)(2,1)S(1)}, bf16[576,128]{1,0:T(8,128)(2,1)S(1)}, u32[]{:S(2)}, u32[]{:S(2)}) collective-permute-start(bf16[576,128]{1,0:T(8,128)(2,1)S(1)} %get-tuple-element.14), channel_id=1, source_target_pairs={{0,6},{2,4},{4,2},{6,0},{8,14},{10,12},{12,10},{14,8},{1,7},{3,5},... | collective-permute-start | bytes 442376 | tf_op jit(solution)/shard_map/ppermute | solution.py:161
  14.8 8.5 %collective-permute-start.4 = (bf16[576,128]{1,0:T(8,128)(2,1)S(1)}, bf16[576,128]{1,0:T(8,128)(2,1)S(1)}, u32[]{:S(2)}, u32[]{:S(2)}) collective-permute-start(bf16[576,128]{1,0:T(8,128)(2,1)S(1)} %get-tuple-element.16), channel_id=1, source_target_pairs={{0,2},{2,0},{4,6},{6,4},{8,10},{10,8},{12,14},{14,12},{1,3},{3,1},... | collective-permute-start | bytes 442376 | tf_op jit(solution)/shard_map/ppermute | solution.py:161
  16.7 9.9 %collective-permute-start.5 = (bf16[576,128]{1,0:T(8,128)(2,1)S(1)}, bf16[576,128]{1,0:T(8,128)(2,1)S(1)}, u32[]{:S(2)}, u32[]{:S(2)}) collective-permute-start(bf16[576,128]{1,0:T(8,128)(2,1)S(1)} %get-tuple-element.18), channel_id=1, source_target_pairs={{0,4},{2,6},{4,0},{6,2},{8,12},{10,14},{12,8},{14,10},{1,5},{3,7},... | collective-permute-start | bytes 442376 | tf_op jit(solution)/shard_map/ppermute | solution.py:161
  20.1 7.4 %collective-permute-start.6 = (bf16[576,128]{1,0:T(8,128)(2,1)S(1)}, bf16[576,128]{1,0:T(8,128)(2,1)S(1)}, u32[]{:S(2)}, u32[]{:S(2)}) collective-permute-start(bf16[576,128]{1,0:T(8,128)(2,1)S(1)} %get-tuple-element.17), channel_id=1, source_target_pairs={{0,6},{2,4},{4,2},{6,0},{8,14},{10,12},{12,10},{14,8},{1,7},{3,5},... | collective-permute-start | bytes 442376 | tf_op jit(solution)/shard_map/ppermute | solution.py:161
  20.2 9.7 %collective-permute-start.14 = (bf16[576,128]{1,0:T(8,128)(2,1)S(1)}, bf16[576,128]{1,0:T(8,128)(2,1)S(1)}, u32[]{:S(2)}, u32[]{:S(2)}) collective-permute-start(bf16[576,128]{1,0:T(8,128)(2,1)S(1)} %add_convert_fusion), channel_id=1, source_target_pairs={{0,8},{2,10},{4,12},{6,14},{8,0},{10,2},{12,4},{14,6},{1,9},{3,11}... | collective-permute-start | bytes 442376 | tf_op jit(solution)/shard_map/ppermute | solution.py:161
  27.7 9.7 %collective-permute-start.7 = (bf16[576,128]{1,0:T(8,128)(2,1)S(1)}, bf16[576,128]{1,0:T(8,128)(2,1)S(1)}, u32[]{:S(2)}, u32[]{:S(2)}) collective-permute-start(bf16[576,128]{1,0:T(8,128)(2,1)S(1)} %add_convert_fusion.1), channel_id=1, source_target_pairs={{0,8},{2,10},{4,12},{6,14},{8,0},{10,2},{12,4},{14,6},{1,9},{3,11}... | collective-permute-start | bytes 442376 | tf_op jit(solution)/shard_map/ppermute | solution.py:161
  30.1 9.7 %collective-permute-start.15 = (bf16[576,128]{1,0:T(8,128)(2,1)S(1)}, bf16[576,128]{1,0:T(8,128)(2,1)S(1)}, u32[]{:S(2)}, u32[]{:S(2)}) collective-permute-start(bf16[576,128]{1,0:T(8,128)(2,1)S(1)} %get-tuple-element.10), channel_id=1, source_target_pairs={{0,2},{2,0},{4,6},{6,4},{8,10},{10,8},{12,14},{14,12},{1,3},{3,1},... | collective-permute-start | bytes 442376 | tf_op jit(solution)/shard_map/ppermute | solution.py:161
  31.3 10.0 %collective-permute-start.16 = (bf16[576,128]{1,0:T(8,128)(2,1)S(1)}, bf16[576,128]{1,0:T(8,128)(2,1)S(1)}, u32[]{:S(2)}, u32[]{:S(2)}) collective-permute-start(bf16[576,128]{1,0:T(8,128)(2,1)S(1)} %get-tuple-element.10), channel_id=1, source_target_pairs={{0,4},{2,6},{4,0},{6,2},{8,12},{10,14},{12,8},{14,10},{1,5},{3,7},... | collective-permute-start | bytes 442376 | tf_op jit(solution)/shard_map/ppermute | solution.py:161
  34.0 9.3 %collective-permute-start.17 = (bf16[576,128]{1,0:T(8,128)(2,1)S(1)}, bf16[576,128]{1,0:T(8,128)(2,1)S(1)}, u32[]{:S(2)}, u32[]{:S(2)}) collective-permute-start(bf16[576,128]{1,0:T(8,128)(2,1)S(1)} %get-tuple-element.10), channel_id=1, source_target_pairs={{0,6},{2,4},{4,2},{6,0},{8,14},{10,12},{12,10},{14,8},{1,7},{3,5},... | collective-permute-start | bytes 442376 | tf_op jit(solution)/shard_map/ppermute | solution.py:161
  37.5 8.8 %collective-permute-start.8 = (bf16[576,128]{1,0:T(8,128)(2,1)S(1)}, bf16[576,128]{1,0:T(8,128)(2,1)S(1)}, u32[]{:S(2)}, u32[]{:S(2)}) collective-permute-start(bf16[576,128]{1,0:T(8,128)(2,1)S(1)} %get-tuple-element.12), channel_id=1, source_target_pairs={{0,2},{2,0},{4,6},{6,4},{8,10},{10,8},{12,14},{14,12},{1,3},{3,1},... | collective-permute-start | bytes 442376 | tf_op jit(solution)/shard_map/ppermute | solution.py:161
  39.8 6.8 %collective-permute-start.9 = (bf16[576,128]{1,0:T(8,128)(2,1)S(1)}, bf16[576,128]{1,0:T(8,128)(2,1)S(1)}, u32[]{:S(2)}, u32[]{:S(2)}) collective-permute-start(bf16[576,128]{1,0:T(8,128)(2,1)S(1)} %get-tuple-element.12), channel_id=1, source_target_pairs={{0,4},{2,6},{4,0},{6,2},{8,12},{10,14},{12,8},{14,10},{1,5},{3,7},... | collective-permute-start | bytes 442376 | tf_op jit(solution)/shard_map/ppermute | solution.py:161
  39.8 9.1 %collective-permute-start.10 = (bf16[576,128]{1,0:T(8,128)(2,1)S(1)}, bf16[576,128]{1,0:T(8,128)(2,1)S(1)}, u32[]{:S(2)}, u32[]{:S(2)}) collective-permute-start(bf16[576,128]{1,0:T(8,128)(2,1)S(1)} %get-tuple-element.12), channel_id=1, source_target_pairs={{0,6},{2,4},{4,2},{6,0},{8,14},{10,12},{12,10},{14,8},{1,7},{3,5},... | collective-permute-start | bytes 442376 | tf_op jit(solution)/shard_map/ppermute | solution.py:161
  43.4 5.5 %copy-start.5 = (bf16[2304,128]{1,0:T(8,128)(2,1)}, bf16[2304,128]{1,0:T(8,128)(2,1)S(1)}, u32[]{:S(2)}) copy-start(bf16[2304,128]{1,0:T(8,128)(2,1)S(1)} %constant_dynamic-update-slice_fusion) | copy-start | bytes 1769476
  48.9 0.8 %copy-start.4 = (bf16[2304,128]{1,0:T(8,128)(2,1)}, bf16[2304,128]{1,0:T(8,128)(2,1)S(1)}, u32[]{:S(2)}) copy-start(bf16[2304,128]{1,0:T(8,128)(2,1)S(1)} %constant_dynamic-update-slice_fusion.4) | copy-start | bytes 1769476

commit v5 on v3

--- a/solution.py
+++ b/solution.py
@@ -170,9 +170,13 @@
         assert devices == 1 << bits
         self.near = min(4, devices)
         self.far = [1 << k for k in range(self.near.bit_length() - 1, bits)]
+        if len(self.far) and self.near == 4:
+            self.far[0] = 6
         self.rows = value.shape[0] // self.near
         self.value, self.scale = value, scale
-        self.at = lax.axis_index("dp") % self.near
+        place_dp = lax.axis_index("dp")
+        mirrored = place_dp ^ (((place_dp >> 2) & 1) << 1) if self.far and self.near == 4 else place_dp
+        self.at = mirrored % self.near
 
     def quarter(self, index):
         return lax.dynamic_slice_in_dim(self.value, index * self.rows, self.rows, 0)

time: 49.9 us -> 49 us (0.982)
  waiting for transfers between devices: 17.8 us -> 13.3 us
  starting transfers between devices: 22.3 us -> 25.9 us
    ppermute x14, waiting for transfers between devices: 15 us -> 10.5 us  [swapped(): return lax.ppermute(value, 'dp', pairs)]
    ppermute x14, starting transfers between devices: 21.2 us -> 24.8 us  [swapped(): return lax.ppermute(value, 'dp', pairs)]
where the time goes in v5:
time: 49 us; the launch traced here: 48.8 us
  starting transfers between devices  25.9 us (53%)
  waiting for transfers between devices  13.3 us (27%)
  Pallas kernels  7.29 us (15%)
  local copies, waits for them, and re-layouts  1.19 us (2%)
  between operations  0.78 us (2%)
    ppermute x14, starting transfers between devices, swapped(): return lax.ppermute(value, 'dp', pairs)  24.8 us
    ppermute x14, waiting for transfers between devices, swapped(): return lax.ppermute(value, 'dp', pairs)  10.5 us
    pallas_call x4, Pallas kernels, call(): pl.pallas_call(functools.partial(kernel, cols), out_shape=outs, in_specs=...  7.29 us
    ppermute x4, waiting for transfers between devices, body(): lax.ppermute(v, 'shard', swap)  2.84 us
    ppermute x4, starting transfers between devices, body(): lax.ppermute(v, 'shard', swap)  1.11 us
  transfers between devices with their start and end apart: 18, of which 9 were waited for; matrix products, arithmetic and copies ran while one was open for 1% of the time, Pallas kernels for 15%

profile of v5, /device:TPU:0, one launch (start us, length us, event | category | flops | bytes accessed | tf_op | source)
XLA Modules:
  0.0 48.8 jit_solution(15583137530075959503)
XLA Ops:
  0.6 0.5 %collective-permute-start.2 = (bf16[2304,128]{1,0:T(8,128)(2,1)}, bf16[2304,128]{1,0:T(8,128)(2,1)S(1)}, u32[]{:S(2)}, u32[]{:S(2)}) collective-permute-start(bf16[2304,128]{1,0:T(8,128)(2,1)} %bitcast.7), channel_id=1, source_target_pairs={{0,1},{1,0},{2,3},{3,2},{4,5},{5,4},{6,7},{7,6},{8,9},{9,8},{10,11... | collective-permute-start | bytes 1769480 | tf_op jit(solution)/shard_map/ppermute | solution.py:228
  1.1 0.1 collective-permute-start.3
  1.2 0.4 collective-permute-start
  1.7 2.5 %collective-permute-done.x_other = bf16[512,256]{1,0:T(8,128)(2,1)S(1)} collective-permute-done((bf16[512,256]{1,0:T(8,128)(2,1)}, bf16[512,256]{1,0:T(8,128)(2,1)S(1)}, u32[]{:S(2)}, u32[]{:S(2)}) %collective-permute-start) | collective-permute-done | bytes 262176 | tf_op jit(solution)/shard_map/ppermute | solution.py:228
  4.2 0.4 collective-permute-done.1.c_other
  4.6 2.9 %shard_map.68 = (bf16[2304,128]{1,0:T(8,128)(2,1)S(1)}, bf16[512,256]{1,0:T(8,128)(2,1)S(1)}, f32[1024,128]{1,0:T(8,128)S(1)}) custom-call(bf16[512,256]{1,0:T(8,128)(2,1)S(1)} %bitcast.16, bf16[512,256]{1,0:T(8,128)(2,1)S(1)} %collective-permute-done.x_other, bf16[512,256]{1,0:T(8,128)(2,1)S(1)} %bitcast.13, ...), custom_call_target="tpu_custom_call" | custom-call | flops 1811939328 | bytes 2232320 | tf_op jit(solution)/shard_map/pallas_call | solution.py:146
  7.6 2.9 %collective-permute-start.11 = (bf16[576,128]{1,0:T(8,128)(2,1)S(1)}, bf16[576,128]{1,0:T(8,128)(2,1)S(1)}, u32[]{:S(2)}, u32[]{:S(2)}) collective-permute-start(bf16[576,128]{1,0:T(8,128)(2,1)S(1)} %get-tuple-element.13), channel_id=1, source_target_pairs={{0,2},{2,0},{4,6},{6,4},{8,10},{10,8},{12,14},{14,12},{1,3},{3,1},... | collective-permute-start | bytes 442376 | tf_op jit(solution)/shard_map/ppermute | solution.py:159
  10.5 1.6 %collective-permute-start.12 = (bf16[576,128]{1,0:T(8,128)(2,1)S(1)}, bf16[576,128]{1,0:T(8,128)(2,1)S(1)}, u32[]{:S(2)}, u32[]{:S(2)}) collective-permute-start(bf16[576,128]{1,0:T(8,128)(2,1)S(1)} %get-tuple-element.15), channel_id=1, source_target_pairs={{0,4},{2,6},{4,0},{6,2},{8,12},{10,14},{12,8},{14,10},{1,5},{3,7},... | collective-permute-start | bytes 442376 | tf_op jit(solution)/shard_map/ppermute | solution.py:159
  12.1 2.6 %shard_map.70 = bf16[2304,128]{1,0:T(8,128)(2,1)S(1)} custom-call(bf16[512,256]{1,0:T(8,128)(2,1)S(1)} %bitcast.17, bf16[512,256]{1,0:T(8,128)(2,1)S(1)} %collective-permute-done.x_other, bf16[512,256]{1,0:T(8,128)(2,1)S(1)} %bitcast.14, bf16[512,256]{1,0:T(8,128)(2,1)S(1)} %collective-permute-done.1.c_other, bf16[2304,128]{1,0:T(8,128)(2,1)S(1)} %bitcast.10, ...), custom_call_target="tpu_custom_call" | custom-call | flops 1207959552 | bytes 2752512 | tf_op jit(solution)/shard_map/pallas_call | solution.py:146
  14.7 2.0 %collective-permute-start.4 = (bf16[576,128]{1,0:T(8,128)(2,1)S(1)}, bf16[576,128]{1,0:T(8,128)(2,1)S(1)}, u32[]{:S(2)}, u32[]{:S(2)}) collective-permute-start(bf16[576,128]{1,0:T(8,128)(2,1)S(1)} %get-tuple-element.16), channel_id=1, source_target_pairs={{0,2},{2,0},{4,6},{6,4},{8,10},{10,8},{12,14},{14,12},{1,3},{3,1},... | collective-permute-start | bytes 442376 | tf_op jit(solution)/shard_map/ppermute | solution.py:159
  16.7 1.6 %collective-permute-start.5 = (bf16[576,128]{1,0:T(8,128)(2,1)S(1)}, bf16[576,128]{1,0:T(8,128)(2,1)S(1)}, u32[]{:S(2)}, u32[]{:S(2)}) collective-permute-start(bf16[576,128]{1,0:T(8,128)(2,1)S(1)} %get-tuple-element.18), channel_id=1, source_target_pairs={{0,4},{2,6},{4,0},{6,2},{8,12},{10,14},{12,8},{14,10},{1,5},{3,7},... | collective-permute-start | bytes 442376 | tf_op jit(solution)/shard_map/ppermute | solution.py:159
  18.3 1.8 %shard_map.69 = bf16[512,256]{1,0:T(8,128)(2,1)} custom-call(bf16[512,256]{1,0:T(8,128)(2,1)S(1)} %bitcast.18, bf16[512,256]{1,0:T(8,128)(2,1)S(1)} %get-tuple-element.6.h_ref, bf16[2304,128]{1,0:T(8,128)(2,1)S(1)} %bitcast.11, bf16[2304,128]{1,0:T(8,128)(2,1)S(1)} %collective-permute-done.3.w_other), custom_call_target="tpu_custom_call" | custom-call | flops 603979776 | bytes 1703936 | tf_op jit(solution)/shard_map/pallas_call | solution.py:146
  20.1 0.1 add_convert_fusion
  20.2 4.1 %collective-permute-start.14 = (bf16[576,128]{1,0:T(8,128)(2,1)S(1)}, bf16[576,128]{1,0:T(8,128)(2,1)S(1)}, u32[]{:S(2)}, u32[]{:S(2)}) collective-permute-start(bf16[576,128]{1,0:T(8,128)(2,1)S(1)} %add_convert_fusion), channel_id=1, source_target_pairs={{0,12},{2,14},{4,8},{6,10},{8,4},{10,6},{12,0},{14,2},{1,13},{3,15... | collective-permute-start | bytes 442376 | tf_op jit(solution)/shard_map/ppermute | solution.py:159
  24.3 1.9 %collective-permute-done.6 = bf16[576,128]{1,0:T(8,128)(2,1)S(1)} collective-permute-done((bf16[576,128]{1,0:T(8,128)(2,1)S(1)}, bf16[576,128]{1,0:T(8,128)(2,1)S(1)}, u32[]{:S(2)}, u32[]{:S(2)}) %collective-permute-start.6) | collective-permute-done | bytes 147488 | tf_op jit(solution)/shard_map/ppermute | solution.py:159
  26.1 0.1 add_convert_fusion.1
  26.2 6.3 %collective-permute-start.7 = (bf16[576,128]{1,0:T(8,128)(2,1)S(1)}, bf16[576,128]{1,0:T(8,128)(2,1)S(1)}, u32[]{:S(2)}, u32[]{:S(2)}) collective-permute-start(bf16[576,128]{1,0:T(8,128)(2,1)S(1)} %add_convert_fusion.1), channel_id=1, source_target_pairs={{0,12},{2,14},{4,8},{6,10},{8,4},{10,6},{12,0},{14,2},{1,13},{3,15... | collective-permute-start | bytes 442376 | tf_op jit(solution)/shard_map/ppermute | solution.py:159
  32.6 0.1 broadcast.7.clone.1
  32.6 0.1 constant_dynamic-update-slice_fusion.3
  32.7 1.6 %collective-permute-start.15 = (bf16[576,128]{1,0:T(8,128)(2,1)S(1)}, bf16[576,128]{1,0:T(8,128)(2,1)S(1)}, u32[]{:S(2)}, u32[]{:S(2)}) collective-permute-start(bf16[576,128]{1,0:T(8,128)(2,1)S(1)} %get-tuple-element.10), channel_id=1, source_target_pairs={{0,2},{2,0},{4,6},{6,4},{8,10},{10,8},{12,14},{14,12},{1,3},{3,1},... | collective-permute-start | bytes 442376 | tf_op jit(solution)/shard_map/ppermute | solution.py:159
  34.3 2.0 %collective-permute-start.17 = (bf16[576,128]{1,0:T(8,128)(2,1)S(1)}, bf16[576,128]{1,0:T(8,128)(2,1)S(1)}, u32[]{:S(2)}, u32[]{:S(2)}) collective-permute-start(bf16[576,128]{1,0:T(8,128)(2,1)S(1)} %get-tuple-element.10), channel_id=1, source_target_pairs={{0,6},{2,4},{4,2},{6,0},{8,14},{10,12},{12,10},{14,8},{1,7},{3,5},... | collective-permute-start | bytes 442376 | tf_op jit(solution)/shard_map/ppermute | solution.py:159
  36.3 0.1 collective-permute-done.7
  36.4 0.1 broadcast.7.clone
  36.5 0.1 constant_dynamic-update-slice_fusion.7
  36.6 2.5 %collective-permute-start.8 = (bf16[576,128]{1,0:T(8,128)(2,1)S(1)}, bf16[576,128]{1,0:T(8,128)(2,1)S(1)}, u32[]{:S(2)}, u32[]{:S(2)}) collective-permute-start(bf16[576,128]{1,0:T(8,128)(2,1)S(1)} %get-tuple-element.12), channel_id=1, source_target_pairs={{0,2},{2,0},{4,6},{6,4},{8,10},{10,8},{12,14},{14,12},{1,3},{3,1},... | collective-permute-start | bytes 442376 | tf_op jit(solution)/shard_map/ppermute | solution.py:159
  39.0 1.2 %collective-permute-done.15 = bf16[576,128]{1,0:T(8,128)(2,1)S(1)} collective-permute-done((bf16[576,128]{1,0:T(8,128)(2,1)S(1)}, bf16[576,128]{1,0:T(8,128)(2,1)S(1)}, u32[]{:S(2)}, u32[]{:S(2)}) %collective-permute-start.15) | collective-permute-done | bytes 147488 | tf_op jit(solution)/shard_map/ppermute | solution.py:159
  40.2 0.3 collective-permute-start.10
  40.6 3.1 %collective-permute-done.17 = bf16[576,128]{1,0:T(8,128)(2,1)S(1)} collective-permute-done((bf16[576,128]{1,0:T(8,128)(2,1)S(1)}, bf16[576,128]{1,0:T(8,128)(2,1)S(1)}, u32[]{:S(2)}, u32[]{:S(2)}) %collective-permute-start.17) | collective-permute-done | bytes 147488 | tf_op jit(solution)/shard_map/ppermute | solution.py:159
  43.8 0.7 %collective-permute-done.8 = bf16[576,128]{1,0:T(8,128)(2,1)S(1)} collective-permute-done((bf16[576,128]{1,0:T(8,128)(2,1)S(1)}, bf16[576,128]{1,0:T(8,128)(2,1)S(1)}, u32[]{:S(2)}, u32[]{:S(2)}) %collective-permute-start.8) | collective-permute-done | bytes 147488 | tf_op jit(solution)/shard_map/ppermute | solution.py:159
  44.6 1.2 %collective-permute-done.9 = bf16[576,128]{1,0:T(8,128)(2,1)S(1)} collective-permute-done((bf16[576,128]{1,0:T(8,128)(2,1)S(1)}, bf16[576,128]{1,0:T(8,128)(2,1)S(1)}, u32[]{:S(2)}, u32[]{:S(2)}) %collective-permute-start.9) | collective-permute-done | bytes 147488 | tf_op jit(solution)/shard_map/ppermute | solution.py:159
  45.8 2.2 %collective-permute-done.10 = bf16[576,128]{1,0:T(8,128)(2,1)S(1)} collective-permute-done((bf16[576,128]{1,0:T(8,128)(2,1)S(1)}, bf16[576,128]{1,0:T(8,128)(2,1)S(1)}, u32[]{:S(2)}, u32[]{:S(2)}) %collective-permute-start.10) | collective-permute-done | bytes 147488 | tf_op jit(solution)/shard_map/ppermute | solution.py:159
  48.0 0.8 %copy-done.4 = bf16[2304,128]{1,0:T(8,128)(2,1)} copy-done((bf16[2304,128]{1,0:T(8,128)(2,1)}, bf16[2304,128]{1,0:T(8,128)(2,1)S(1)}, u32[]{:S(2)}) %copy-start.4) | copy-done | bytes 589848
  (34 shorter events, 0.4 us)
Async XLA Ops:
  0.6 4.0 %collective-permute-start.2 = (bf16[2304,128]{1,0:T(8,128)(2,1)}, bf16[2304,128]{1,0:T(8,128)(2,1)S(1)}, u32[]{:S(2)}, u32[]{:S(2)}) collective-permute-start(bf16[2304,128]{1,0:T(8,128)(2,1)} %bitcast.7), channel_id=1, source_target_pairs={{0,1},{1,0},{2,3},{3,2},{4,5},{5,4},{6,7},{7,6},{8,9},{9,8},{10,11... | collective-permute-start | bytes 1769480 | tf_op jit(solution)/shard_map/ppermute | solution.py:228
  1.1 11.0 %collective-permute-start.3 = (bf16[2304,128]{1,0:T(8,128)(2,1)}, bf16[2304,128]{1,0:T(8,128)(2,1)S(1)}, u32[]{:S(2)}, u32[]{:S(2)}) collective-permute-start(bf16[2304,128]{1,0:T(8,128)(2,1)} %bitcast.9), channel_id=1, source_target_pairs={{0,1},{1,0},{2,3},{3,2},{4,5},{5,4},{6,7},{7,6},{8,9},{9,8},{10,11... | collective-permute-start | bytes 1769480 | tf_op jit(solution)/shard_map/ppermute | solution.py:228
  1.2 3.0 %collective-permute-start = (bf16[512,256]{1,0:T(8,128)(2,1)}, bf16[512,256]{1,0:T(8,128)(2,1)S(1)}, u32[]{:S(2)}, u32[]{:S(2)}) collective-permute-start(bf16[512,256]{1,0:T(8,128)(2,1)} %bitcast.15), channel_id=1, source_target_pairs={{0,1},{1,0},{2,3},{3,2},{4,5},{5,4},{6,7},{7,6},{8,9},{9,8},{10,11... | collective-permute-start | bytes 786440 | tf_op jit(solution)/shard_map/ppermute | solution.py:228
  1.7 2.9 %collective-permute-start.1 = (bf16[512,256]{1,0:T(8,128)(2,1)}, bf16[512,256]{1,0:T(8,128)(2,1)S(1)}, u32[]{:S(2)}, u32[]{:S(2)}) collective-permute-start(bf16[512,256]{1,0:T(8,128)(2,1)} %bitcast.12), channel_id=1, source_target_pairs={{0,1},{1,0},{2,3},{3,2},{4,5},{5,4},{6,7},{7,6},{8,9},{9,8},{10,11... | collective-permute-start | bytes 786440 | tf_op jit(solution)/shard_map/ppermute | solution.py:228
  1.7 2.9 %copy-start = (bf16[9,256,128]{2,1,0:T(8,128)(2,1)S(1)}, bf16[9,256,128]{2,1,0:T(8,128)(2,1)}, u32[]{:S(2)}) copy-start(bf16[9,256,128]{2,1,0:T(8,128)(2,1)} %param.6) | copy-start | bytes 1769476
  1.7 2.9 %copy-start.2 = (bf16[1,16,32,256]{3,2,1,0:T(8,128)(2,1)S(1)}, bf16[1,16,32,256]{3,2,1,0:T(8,128)(2,1)}, u32[]{:S(2)}) copy-start(bf16[1,16,32,256]{3,2,1,0:T(8,128)(2,1)} %param.5) | copy-start | bytes 786436
  1.7 2.9 %copy-start.3 = (bf16[1,16,32,256]{3,2,1,0:T(8,128)(2,1)S(1)}, bf16[1,16,32,256]{3,2,1,0:T(8,128)(2,1)}, u32[]{:S(2)}) copy-start(bf16[1,16,32,256]{3,2,1,0:T(8,128)(2,1)} %param.4) | copy-start | bytes 786436
  7.5 4.6 %copy-start.1 = (bf16[9,256,128]{2,1,0:T(8,128)(2,1)S(1)}, bf16[9,256,128]{2,1,0:T(8,128)(2,1)}, u32[]{:S(2)}) copy-start(bf16[9,256,128]{2,1,0:T(8,128)(2,1)} %param.7) | copy-start | bytes 1769476
  7.6 12.5 %collective-permute-start.11 = (bf16[576,128]{1,0:T(8,128)(2,1)S(1)}, bf16[576,128]{1,0:T(8,128)(2,1)S(1)}, u32[]{:S(2)}, u32[]{:S(2)}) collective-permute-start(bf16[576,128]{1,0:T(8,128)(2,1)S(1)} %get-tuple-element.13), channel_id=1, source_target_pairs={{0,2},{2,0},{4,6},{6,4},{8,10},{10,8},{12,14},{14,12},{1,3},{3,1},... | collective-permute-start | bytes 442376 | tf_op jit(solution)/shard_map/ppermute | solution.py:159
  10.5 9.6 %collective-permute-start.12 = (bf16[576,128]{1,0:T(8,128)(2,1)S(1)}, bf16[576,128]{1,0:T(8,128)(2,1)S(1)}, u32[]{:S(2)}, u32[]{:S(2)}) collective-permute-start(bf16[576,128]{1,0:T(8,128)(2,1)S(1)} %get-tuple-element.15), channel_id=1, source_target_pairs={{0,4},{2,6},{4,0},{6,2},{8,12},{10,14},{12,8},{14,10},{1,5},{3,7},... | collective-permute-start | bytes 442376 | tf_op jit(solution)/shard_map/ppermute | solution.py:159
  12.1 8.0 %collective-permute-start.13 = (bf16[576,128]{1,0:T(8,128)(2,1)S(1)}, bf16[576,128]{1,0:T(8,128)(2,1)S(1)}, u32[]{:S(2)}, u32[]{:S(2)}) collective-permute-start(bf16[576,128]{1,0:T(8,128)(2,1)S(1)} %get-tuple-element.14), channel_id=1, source_target_pairs={{0,6},{2,4},{4,2},{6,0},{8,14},{10,12},{12,10},{14,8},{1,7},{3,5},... | collective-permute-start | bytes 442376 | tf_op jit(solution)/shard_map/ppermute | solution.py:159
  14.7 9.5 %collective-permute-start.4 = (bf16[576,128]{1,0:T(8,128)(2,1)S(1)}, bf16[576,128]{1,0:T(8,128)(2,1)S(1)}, u32[]{:S(2)}, u32[]{:S(2)}) collective-permute-start(bf16[576,128]{1,0:T(8,128)(2,1)S(1)} %get-tuple-element.16), channel_id=1, source_target_pairs={{0,2},{2,0},{4,6},{6,4},{8,10},{10,8},{12,14},{14,12},{1,3},{3,1},... | collective-permute-start | bytes 442376 | tf_op jit(solution)/shard_map/ppermute | solution.py:159
  16.7 7.6 %collective-permute-start.5 = (bf16[576,128]{1,0:T(8,128)(2,1)S(1)}, bf16[576,128]{1,0:T(8,128)(2,1)S(1)}, u32[]{:S(2)}, u32[]{:S(2)}) collective-permute-start(bf16[576,128]{1,0:T(8,128)(2,1)S(1)} %get-tuple-element.18), channel_id=1, source_target_pairs={{0,4},{2,6},{4,0},{6,2},{8,12},{10,14},{12,8},{14,10},{1,5},{3,7},... | collective-permute-start | bytes 442376 | tf_op jit(solution)/shard_map/ppermute | solution.py:159
  20.1 6.1 %collective-permute-start.6 = (bf16[576,128]{1,0:T(8,128)(2,1)S(1)}, bf16[576,128]{1,0:T(8,128)(2,1)S(1)}, u32[]{:S(2)}, u32[]{:S(2)}) collective-permute-start(bf16[576,128]{1,0:T(8,128)(2,1)S(1)} %get-tuple-element.17), channel_id=1, source_target_pairs={{0,6},{2,4},{4,2},{6,0},{8,14},{10,12},{12,10},{14,8},{1,7},{3,5},... | collective-permute-start | bytes 442376 | tf_op jit(solution)/shard_map/ppermute | solution.py:159
  20.2 12.4 %collective-permute-start.14 = (bf16[576,128]{1,0:T(8,128)(2,1)S(1)}, bf16[576,128]{1,0:T(8,128)(2,1)S(1)}, u32[]{:S(2)}, u32[]{:S(2)}) collective-permute-start(bf16[576,128]{1,0:T(8,128)(2,1)S(1)} %add_convert_fusion), channel_id=1, source_target_pairs={{0,12},{2,14},{4,8},{6,10},{8,4},{10,6},{12,0},{14,2},{1,13},{3,15... | collective-permute-start | bytes 442376 | tf_op jit(solution)/shard_map/ppermute | solution.py:159
  26.2 10.2 %collective-permute-start.7 = (bf16[576,128]{1,0:T(8,128)(2,1)S(1)}, bf16[576,128]{1,0:T(8,128)(2,1)S(1)}, u32[]{:S(2)}, u32[]{:S(2)}) collective-permute-start(bf16[576,128]{1,0:T(8,128)(2,1)S(1)} %add_convert_fusion.1), channel_id=1, source_target_pairs={{0,12},{2,14},{4,8},{6,10},{8,4},{10,6},{12,0},{14,2},{1,13},{3,15... | collective-permute-start | bytes 442376 | tf_op jit(solution)/shard_map/ppermute | solution.py:159
  32.7 7.5 %collective-permute-start.15 = (bf16[576,128]{1,0:T(8,128)(2,1)S(1)}, bf16[576,128]{1,0:T(8,128)(2,1)S(1)}, u32[]{:S(2)}, u32[]{:S(2)}) collective-permute-start(bf16[576,128]{1,0:T(8,128)(2,1)S(1)} %get-tuple-element.10), channel_id=1, source_target_pairs={{0,2},{2,0},{4,6},{6,4},{8,10},{10,8},{12,14},{14,12},{1,3},{3,1},... | collective-permute-start | bytes 442376 | tf_op jit(solution)/shard_map/ppermute | solution.py:159
  34.3 6.3 %collective-permute-start.16 = (bf16[576,128]{1,0:T(8,128)(2,1)S(1)}, bf16[576,128]{1,0:T(8,128)(2,1)S(1)}, u32[]{:S(2)}, u32[]{:S(2)}) collective-permute-start(bf16[576,128]{1,0:T(8,128)(2,1)S(1)} %get-tuple-element.10), channel_id=1, source_target_pairs={{0,4},{2,6},{4,0},{6,2},{8,12},{10,14},{12,8},{14,10},{1,5},{3,7},... | collective-permute-start | bytes 442376 | tf_op jit(solution)/shard_map/ppermute | solution.py:159
  34.3 9.5 %collective-permute-start.17 = (bf16[576,128]{1,0:T(8,128)(2,1)S(1)}, bf16[576,128]{1,0:T(8,128)(2,1)S(1)}, u32[]{:S(2)}, u32[]{:S(2)}) collective-permute-start(bf16[576,128]{1,0:T(8,128)(2,1)S(1)} %get-tuple-element.10), channel_id=1, source_target_pairs={{0,6},{2,4},{4,2},{6,0},{8,14},{10,12},{12,10},{14,8},{1,7},{3,5},... | collective-permute-start | bytes 442376 | tf_op jit(solution)/shard_map/ppermute | solution.py:159
  36.6 8.0 %collective-permute-start.8 = (bf16[576,128]{1,0:T(8,128)(2,1)S(1)}, bf16[576,128]{1,0:T(8,128)(2,1)S(1)}, u32[]{:S(2)}, u32[]{:S(2)}) collective-permute-start(bf16[576,128]{1,0:T(8,128)(2,1)S(1)} %get-tuple-element.12), channel_id=1, source_target_pairs={{0,2},{2,0},{4,6},{6,4},{8,10},{10,8},{12,14},{14,12},{1,3},{3,1},... | collective-permute-start | bytes 442376 | tf_op jit(solution)/shard_map/ppermute | solution.py:159
  39.0 6.8 %collective-permute-start.9 = (bf16[576,128]{1,0:T(8,128)(2,1)S(1)}, bf16[576,128]{1,0:T(8,128)(2,1)S(1)}, u32[]{:S(2)}, u32[]{:S(2)}) collective-permute-start(bf16[576,128]{1,0:T(8,128)(2,1)S(1)} %get-tuple-element.12), channel_id=1, source_target_pairs={{0,4},{2,6},{4,0},{6,2},{8,12},{10,14},{12,8},{14,10},{1,5},{3,7},... | collective-permute-start | bytes 442376 | tf_op jit(solution)/shard_map/ppermute | solution.py:159
  40.2 7.8 %collective-permute-start.10 = (bf16[576,128]{1,0:T(8,128)(2,1)S(1)}, bf16[576,128]{1,0:T(8,128)(2,1)S(1)}, u32[]{:S(2)}, u32[]{:S(2)}) collective-permute-start(bf16[576,128]{1,0:T(8,128)(2,1)S(1)} %get-tuple-element.12), channel_id=1, source_target_pairs={{0,6},{2,4},{4,2},{6,0},{8,14},{10,12},{12,10},{14,8},{1,7},{3,5},... | collective-permute-start | bytes 442376 | tf_op jit(solution)/shard_map/ppermute | solution.py:159
  43.8 4.2 %copy-start.5 = (bf16[2304,128]{1,0:T(8,128)(2,1)}, bf16[2304,128]{1,0:T(8,128)(2,1)S(1)}, u32[]{:S(2)}) copy-start(bf16[2304,128]{1,0:T(8,128)(2,1)S(1)} %constant_dynamic-update-slice_fusion) | copy-start | bytes 1769476
  48.0 0.8 %copy-start.4 = (bf16[2304,128]{1,0:T(8,128)(2,1)}, bf16[2304,128]{1,0:T(8,128)(2,1)S(1)}, u32[]{:S(2)}) copy-start(bf16[2304,128]{1,0:T(8,128)(2,1)S(1)} %constant_dynamic-update-slice_fusion.4) | copy-start | bytes 1769476
